TPU v7x, 32 devices: a whole 2x2x4 slice. The times are simulated.
32 devices in a mesh: dp: 8 (over z, y), section: 4 (over x, core).
Axes of the slice: x: 2, y: 2, z: 4, core: 2. Of those that a mesh axis runs over, the one named last changes fastest.
Arguments:
- held: bfloat16 [4, 1024, 4096], P('section', 'dp'), may hold values from -6 to 6
- norm_gain: bfloat16 [4, 1, 4096], P('section'), may hold values from 0.099609375 to 1.8984375
- w_gate: bfloat16 [4, 1, 4096, 6144], P('section', None, None, 'dp'), may hold values from -0.09375 to 0.09375
- w_up: bfloat16 [4, 1, 4096, 6144], P('section', None, None, 'dp'), may hold values from -0.09375 to 0.09375
- w_down: bfloat16 [4, 1, 6144, 4096], P('section', None, 'dp'), may hold values from -0.078125 to 0.078125
- layer_counts: int32 [4], P('section'), may hold values from 0 to 1, as said below
- query_bank: bfloat16 [128, 4096], P('dp'), may hold values from -0.099609375 to 0.099609375
- pin_bank: bfloat16 [128, 4096], P('dp'), may hold values from -0.099609375 to 0.099609375
- positive: int32 [128], P('dp'), may hold values from 0 to 127, each once
Outputs:
- section_out: bfloat16 [4, 1024, 4096], P('section', 'dp')
- grad_query: float32 [128, 4096], P('dp', 'section')
- grad_pin: float32 [128, 4096], P('dp', 'section')
Inputs may be any that keep to these rules, and one draw needn't show every extreme that they name: `layer_counts`: each section's number of applied layer slots; some section applies 1 and some section applies none. Each pin is the positive of exactly one query.
All inputs are finite; a program needn't handle non-finite values.
Results may differ from a plain program's by a relative error of at most 0.012.
Values may be sent and summed in bfloat16 or wider, within the bound.
No kernel may reach another device: no remote copies, remote signals or barrier semaphores. Data moves between devices by JAX's collectives and lax.ppermute only.
A program may use at most 128 MiB of HBM per device.

v0:
```python
import functools

import jax
import jax.numpy as jnp
from jax import lax
from jax.experimental import pallas as pl
from jax.experimental.pallas import tpu as pltpu
from jax.sharding import PartitionSpec as P

INV_TEMP = 20.0
EPSILON = 1e-06
BOTH = ("dp", "section")
ANYWHERE = pl.BlockSpec(memory_space=pl.ANY)
IN_VMEM = pl.BlockSpec(memory_space=pltpu.VMEM)


def ring_order(size):
    return list(range(0, size, 2)) + list(range(size - 1, 0, -2))


def rms_scaled(stream, gain_row):
    values = stream.astype(jnp.float32)
    factor = lax.rsqrt(jnp.mean(values * values, axis=-1, keepdims=True) + EPSILON)
    return (values * factor * gain_row.astype(jnp.float32)).astype(jnp.bfloat16)


def unit_rows(values):
    floats = values.astype(jnp.float32)
    length = jnp.sqrt(jnp.sum(floats * floats, axis=-1, keepdims=True) + EPSILON)
    return (floats / length, length)


def copies_in(pieces, tokens, sems):
    rows = pieces[0].shape[0]
    copies = [
        pltpu.make_async_copy(piece, tokens.at[pl.ds(i * rows, rows)], sems.at[i])
        for i, piece in enumerate(pieces)
    ]
    for copy in copies:
        copy.start()
    return copies


def copies_out(result, outs, sems):
    rows = outs[0].shape[0]
    copies = [
        pltpu.make_async_copy(result.at[pl.ds(i * rows, rows)], out, sems.at[i])
        for i, out in enumerate(outs)
    ]
    for copy in copies:
        copy.start()
    for copy in copies:
        copy.wait()


def gated(tokens, gate, up, hidden):
    gate_out = jnp.dot(tokens[...], gate[...], preferred_element_type=jnp.float32)
    up_out = jnp.dot(tokens[...], up[...], preferred_element_type=jnp.float32)
    hidden[...] = (gate_out / (1 + jnp.exp(-gate_out)) * up_out).astype(jnp.bfloat16)


def lowered(hidden, down, result):
    result[...] = jnp.dot(hidden[...], down[...], preferred_element_type=jnp.float32).astype(
        jnp.bfloat16
    )


def last_rows(result, count, tails):
    rows = result.shape[0] // count
    for i in range(count):
        end = result[(i + 1) * rows - 16 : (i + 1) * rows].astype(jnp.float32)
        tails[i : i + 1] = end[15:]


def first_kernel(count, *refs):
    pieces, weights, refs = refs[:count], refs[count : count + 3], refs[count + 3 :]
    outs, tails, kept, refs = refs[:count], refs[count], refs[count + 1 : count + 4], refs[count + 4 :]
    tokens, hidden, result, in_sems, out_sems, weight_sems = refs
    loads = copies_in(pieces, tokens, in_sems)
    fetches = [
        pltpu.make_async_copy(weight, keep, weight_sems.at[i])
        for i, (weight, keep) in enumerate(zip(weights, kept))
    ]
    for copy in fetches:
        copy.start()
    for copy in loads + fetches[:2]:
        copy.wait()
    gated(tokens, kept[0], kept[1], hidden)
    fetches[2].wait()
    lowered(hidden, kept[2], result)
    last_rows(result, count, tails)
    copies_out(result, outs, out_sems)


def next_kernel(count, *refs):
    pieces, weights, refs = refs[:count], refs[count : count + 3], refs[count + 3 :]
    outs, tails, refs = refs[:count], refs[count], refs[count + 1 :]
    tokens, hidden, result, in_sems, out_sems = refs
    for copy in copies_in(pieces, tokens, in_sems):
        copy.wait()
    gated(tokens, weights[0], weights[1], hidden)
    lowered(hidden, weights[2], result)
    last_rows(result, count, tails)
    copies_out(result, outs, out_sems)


def multiply(pieces, weights, keep):
    count = len(pieces)
    rows, width = pieces[0].shape
    units = weights[0].shape[1]
    scratch = [
        pltpu.VMEM((count * rows, width), jnp.bfloat16),
        pltpu.VMEM((count * rows, units), jnp.bfloat16),
        pltpu.VMEM((count * rows, width), jnp.bfloat16),
        pltpu.SemaphoreType.DMA((count,)),
        pltpu.SemaphoreType.DMA((count,)),
    ]
    out_shape = [jax.ShapeDtypeStruct(p.shape, jnp.bfloat16) for p in pieces]
    out_shape += [jax.ShapeDtypeStruct((8, width), jnp.float32)]
    params = pltpu.CompilerParams(vmem_limit_bytes=20 << 20)
    tokens = count * rows
    cost = pl.CostEstimate(
        flops=6 * tokens * width * units, bytes_accessed=4 * tokens * width, transcendentals=0
    )
    if keep:
        outs = pl.pallas_call(
            functools.partial(first_kernel, count),
            out_shape=out_shape + [pltpu.VMEM(w.shape, w.dtype) for w in weights],
            in_specs=[ANYWHERE] * (count + 3),
            out_specs=[ANYWHERE] * count + [IN_VMEM] * 4,
            scratch_shapes=scratch + [pltpu.SemaphoreType.DMA((3,))],
            compiler_params=params,
            cost_estimate=cost,
        )(*pieces, *weights)
        return outs[:count], outs[count], outs[count + 1 :]
    weights = [pltpu.with_memory_space_constraint(w, pltpu.VMEM) for w in weights]
    outs = pl.pallas_call(
        functools.partial(next_kernel, count),
        out_shape=out_shape,
        in_specs=[ANYWHERE] * count + [IN_VMEM] * 3,
        out_specs=[ANYWHERE] * count + [IN_VMEM],
        scratch_shapes=scratch,
        compiler_params=params,
        cost_estimate=cost,
    )(*pieces, *weights)
    return outs[:count], outs[count]


def sum_kernel(plan, sources, *refs):
    ins, outs, (loaded, result, in_sems, out_sems) = refs[:sources], refs[sources:-4], refs[-4:]
    rows = result.shape[1]
    part = rows // 2
    groups, slot = [], 0
    for group, (terms, out, out_row) in enumerate(plan):
        for cut in range(2):
            copies = []
            for i, (source, row) in enumerate(terms):
                copies.append(
                    pltpu.make_async_copy(
                        ins[source].at[pl.ds(row + cut * part, part)],
                        loaded.at[slot + i, pl.ds(cut * part, part)],
                        in_sems.at[2 * (slot + i) + cut],
                    )
                )
            groups.append((group, cut, slot, copies, out, out_row))
        slot += len(terms)
    for entry in groups:
        for copy in entry[3]:
            copy.start()
    stores = []
    for group, cut, slot, copies, out, out_row in groups:
        for copy in copies:
            copy.wait()
        here = slice(cut * part, (cut + 1) * part)
        total = loaded[slot, here].astype(jnp.float32)
        for i in range(1, len(copies)):
            total = total + loaded[slot + i, here].astype(jnp.float32)
        result[group, here] = total.astype(jnp.bfloat16)
        store = pltpu.make_async_copy(
            result.at[group, pl.ds(cut * part, part)],
            outs[out].at[pl.ds(out_row + cut * part, part)],
            out_sems.at[2 * group + cut],
        )
        store.start()
        stores.append(store)
    for store in stores:
        store.wait()


def sums(plan, sources, rows, out_shapes):
    terms = sum(len(entry[0]) for entry in plan)
    width = sources[0].shape[1]
    return pl.pallas_call(
        functools.partial(sum_kernel, plan, len(sources)),
        out_shape=[jax.ShapeDtypeStruct(shape, jnp.bfloat16) for shape in out_shapes],
        in_specs=[ANYWHERE] * len(sources),
        out_specs=[ANYWHERE] * len(out_shapes),
        scratch_shapes=[
            pltpu.VMEM((terms, rows, width), jnp.bfloat16),
            pltpu.VMEM((len(plan), rows, width), jnp.bfloat16),
            pltpu.SemaphoreType.DMA((2 * terms,)),
            pltpu.SemaphoreType.DMA((2 * len(plan),)),
        ],
        compiler_params=pltpu.CompilerParams(vmem_limit_bytes=16 << 20),
        cost_estimate=pl.CostEstimate(
            flops=terms * rows * width, bytes_accessed=4 * terms * rows * width, transcendentals=0
        ),
    )(*sources)


def two_sums(first, second):
    shape = first[0].shape
    plan = (((((0, 0), (1, 0))), 0, 0), ((((2, 0), (3, 0))), 1, 0))
    return sums(plan, [*first, *second], shape[0], [shape, shape])


def loss_kernel(offsets, replicas, pair_dev, where_ref, *refs):
    unit_refs, refs = refs[:-7], refs[-7:]
    fresh_ref, other_ref, target_ref, query_ref, pin_ref, grad_query, grad_pin = refs
    me, section = where_ref[0], where_ref[1]
    sections = len(offsets)
    width = grad_query.shape[1]
    pairs = replicas * pair_dev

    def numbers(shape, dim):
        return lax.broadcasted_iota(jnp.int32, shape, dim)

    units = []
    for ref in unit_refs:
        count = ref.shape[0] // (2 * pairs)
        units += [ref.at[pl.ds(2 * pairs * i, 2 * pairs)] for i in range(count)]

    fresh = fresh_ref[...] + other_ref[other_ref.shape[0] - fresh_ref.shape[0] :]
    row = numbers((sections * replicas, 1), 0)
    source = (me ^ (row % replicas)) * sections
    for j, offset in enumerate(offsets):
        source = source + jnp.where(row // replicas == j, section ^ offset, 0)
    pick = (source == numbers((1, sections * replicas), 1)).astype(jnp.float32)
    fresh = jnp.dot(pick.astype(jnp.bfloat16), fresh, preferred_element_type=jnp.float32)
    squares = jnp.sum(fresh * fresh, axis=1, keepdims=True)
    squares = sum(squares[j * replicas : (j + 1) * replicas] for j in range(sections))
    fresh_length = jnp.sqrt(squares + EPSILON)

    pair = numbers((pairs, 1), 0)
    first = pair % pair_dev == 0
    spread = (pair // pair_dev == numbers((1, replicas), 1)).astype(jnp.float32)
    spread = spread.astype(jnp.bfloat16)
    cosines = jnp.zeros((pairs, pairs), jnp.float32)
    for j in range(sections):
        unit = fresh[j * replicas : (j + 1) * replicas] / fresh_length
        placed = jnp.dot(spread, unit.astype(jnp.bfloat16), preferred_element_type=jnp.float32)
        pins = jnp.where(first, placed, units[j][pairs:].astype(jnp.float32)).astype(jnp.bfloat16)
        if j == 0:
            own_unit, own_pins = unit[:1], pins
        cosines = cosines + lax.dot_general(
            units[j][:pairs], pins, (((1,), (1,)), ((), ())), preferred_element_type=jnp.float32
        )
    raised = jnp.exp(INV_TEMP * cosines - INV_TEMP)
    probs = raised / jnp.sum(raised, axis=1, keepdims=True)
    column = numbers((1, pairs), 1)
    pin_number = (me ^ (column // pair_dev)) * pair_dev + column % pair_dev
    onehot = (pin_number == target_ref[...]).astype(jnp.float32)
    weights = ((probs - onehot) * INV_TEMP).astype(jnp.bfloat16)
    floats = weights.astype(jnp.float32)
    dots = floats * cosines
    query_dot = jnp.sum(dots[:pair_dev], axis=1, keepdims=True)
    pin_dot = jnp.sum(dots.T[:pair_dev], axis=1, keepdims=True)
    query_step = jnp.dot(weights[:pair_dev], own_pins, preferred_element_type=jnp.float32)
    pin_step = jnp.dot(
        floats.T[:pair_dev].astype(jnp.bfloat16),
        units[0][:pairs],
        preferred_element_type=jnp.float32,
    )
    columns = pl.ds(pl.multiple_of(section * width, 128), width)
    for ref, step, dot, grad, fresh_first in (
        (query_ref, query_step, query_dot, grad_query, False),
        (pin_ref, pin_step, pin_dot, grad_pin, True),
    ):
        whole = ref[...].astype(jnp.float32)
        length = jnp.sqrt(jnp.sum(whole * whole, axis=1, keepdims=True) + EPSILON)
        unit = ref[:, columns].astype(jnp.float32) / length
        if fresh_first:
            is_first = numbers((pair_dev, 1), 0) == 0
            length = jnp.where(is_first, fresh_length[:1], length)
            unit = jnp.where(is_first, own_unit, unit)
        grad[...] = (step - unit * dot) / length


def local(held, norm_gain, w_gate, w_up, w_down, layer_counts, query_bank, pin_bank, positive):
    replicas = lax.axis_size("dp")
    sections = lax.axis_size("section")
    rows_dev, model_width = held.shape[1:]
    pair_dev = query_bank.shape[0]
    half = replicas // 2
    cut = rows_dev // 2
    order = ring_order(replicas)
    place = [order.index(replica) for replica in range(replicas)]
    ring = [(order[i], order[(i + 1) % replicas]) for i in range(replicas)]
    ring_back = [(b, a) for a, b in ring]
    me = lax.axis_index("dp")
    section = lax.axis_index("section")
    position = jnp.where(me % 2 == 0, me // 2, replicas - (me + 1) // 2)
    turn = (replicas - position).astype(jnp.uint32)
    last = sections - 1
    active = layer_counts[0] > 0
    stream = held[0]
    col_width = model_width // sections
    col_start = (section * col_width).astype(jnp.uint32)
    turn, position, col_start = lax.optimization_barrier((turn, position, col_start))

    def forward(values):
        return lax.ppermute(values, "dp", ring)

    def backward(values):
        return lax.ppermute(values, "dp", ring_back)

    def own_columns(values):
        return lax.dynamic_slice(values, (jnp.uint32(0), col_start), (values.shape[0], col_width))

    def after(values, others):
        return lax.optimization_barrier((values, others))[0]

    def doubled(values, reach):
        others = lax.ppermute(values, "dp", [(i, i ^ reach) for i in range(replicas)])
        return tuple(jnp.concatenate([v, o], axis=v.ndim - 2) for v, o in zip(values, others))

    def gathered(values, reach):
        while reach < replicas:
            values = doubled(values, reach)
            reach *= 2
        return values

    def added_up(values):
        reach = 1
        while reach < replicas:
            pairs = [(i * sections + last, (i ^ reach) * sections + last) for i in range(replicas)]
            values = values + lax.ppermute(values, BOTH, pairs)
            reach *= 2
        return values

    def with_held(rows):
        rows = jnp.concatenate([rows, rows])
        rows = lax.dynamic_slice(rows, (turn, jnp.uint32(0)), (replicas, model_width))
        mine = jnp.arange(replicas)[:, None] == position
        return rows + jnp.where(mine, stream[rows_dev - 1 :].astype(jnp.float32), 0.0)

    def unit_columns():
        query_send = unit_rows(query_bank)[0].astype(jnp.bfloat16)
        pin_send = unit_rows(pin_bank)[0].astype(jnp.bfloat16)
        return jnp.stack([own_columns(query_send), own_columns(pin_send)]), positive[:, None]

    def gather_and_multiply():
        normed = rms_scaled(stream, norm_gain[0])
        f_top, f_low = normed[:cut], normed[cut:]
        b_top, b_low = f_top, f_low
        f_top, b_low = forward(f_top), backward(b_low)
        f_low, b_top = forward(f_low), backward(b_top)
        own, tails, weights = multiply(
            [normed[:cut], normed[cut:]], [w_gate[0, 0], w_up[0, 0], w_down[0, 0]], True
        )
        sends = doubled(unit_columns(), 1)
        reach = 2
        ready = (own, sends)
        terms_f, terms_b, rows_f, rows_b = [], [], [], [tails[1:2]]
        for step in range(1, half):
            arrived = [f_top, f_low, b_top, b_low]
            f_top, b_low = after((f_top, b_low), ready)
            f_top, b_low = forward(f_top), backward(b_low)
            if step < half - 1:
                f_low, b_top = after((f_low, b_top), ready)
                f_low, b_top = forward(f_low), backward(b_top)
            if reach < replicas:
                sends = doubled(after(sends, arrived), reach)
                reach *= 2
            terms, tails = multiply(arrived, weights, False)
            terms_f.append(terms[:2])
            terms_b.append(terms[2:])
            rows_f.append(tails[1:2])
            rows_b.append(tails[3:4])
            ready = (terms, sends)
        sends = gathered(sends, reach)
        f_low, b_top = forward(terms_b[-1][1]), backward(terms_f[-1][0])
        far, tails = multiply([f_top, b_low], weights, False)
        f_top, b_low = forward(far[0]), backward(far[1])
        rows = jnp.concatenate(rows_b + [tails[1:2]] + rows_f[::-1])
        rows = after(rows, (f_low, b_top))
        fresh = added_up(with_held(rows)).astype(jnp.bfloat16)
        moving = (f_top, f_low, b_top, b_low)
        return tuple(own), tuple(terms_f), tuple(terms_b), moving, fresh, sends

    def gather_only():
        fresh = added_up(with_held(jnp.zeros((replicas, model_width), jnp.float32)))
        empty = jnp.zeros((cut, model_width), jnp.bfloat16)
        some = tuple((empty, empty) for _ in range(1, half))
        return (
            (empty, empty),
            some,
            some,
            (empty,) * 4,
            fresh.astype(jnp.bfloat16),
            gathered(unit_columns(), 1),
        )

    own, terms_f, terms_b, moving, fresh, sends = lax.cond(
        active, gather_and_multiply, gather_only
    )

    sends, targets = sends
    pairs = sends.shape[1]
    fresh = jnp.stack([fresh[place[replica]] for replica in range(replicas)])
    fresh = jnp.where(section == last, fresh, jnp.zeros_like(fresh))
    fresh = fresh.reshape(replicas * sections, col_width)
    units = sends.reshape(2 * pairs, col_width)

    def section_swap(units, fresh, reach):
        message = jnp.concatenate([units, fresh])
        other = lax.ppermute(message, "section", [(s, s ^ reach) for s in range(sections)])
        return other

    offsets = [0, sections // 2]
    other = section_swap(units, fresh, sections // 2)

    def reduce_middle(moving):
        f_top, f_low, b_top, b_low = moving
        for distance in range(half - 1, 1, -1):
            to_f, to_b = terms_b[distance - 1], terms_f[distance - 1]
            if distance < half - 1:
                f_low, b_top = two_sums((to_f[1], f_low), (to_b[0], b_top))
                f_low, b_top = forward(f_low), backward(b_top)
            f_top, b_low = two_sums((to_f[0], f_top), (to_b[1], b_low))
            f_top, b_low = forward(f_top), backward(b_low)
        return f_top, f_low, b_top, b_low

    moving = lax.cond(active, reduce_middle, lambda moving: moving, moving)
    other, moving = lax.optimization_barrier((other, moving))
    units = [units]
    reach = sections // 4
    while reach:
        size = other.shape[0] - fresh.shape[0]
        units, fresh = units + [other[:size]], fresh + other[size:]
        other = section_swap(jnp.concatenate(units), fresh, reach)
        offsets += [offset ^ reach for offset in offsets]
        reach //= 2
    place_here = jnp.stack([me, section])

    def loss(units, fresh, other):
        grad = jax.ShapeDtypeStruct((pair_dev, col_width), jnp.float32)
        return pl.pallas_call(
            functools.partial(loss_kernel, offsets, replicas, pair_dev),
            out_shape=[grad, grad],
            in_specs=[pl.BlockSpec(memory_space=pltpu.SMEM)] + [IN_VMEM] * (len(units) + 6),
            out_specs=[IN_VMEM] * 2,
            compiler_params=pltpu.CompilerParams(vmem_limit_bytes=32 << 20),
        )(place_here, *units, other, fresh, other, targets, query_bank, pin_bank)

    def reduce_last(moving, units, fresh, other):
        f_top, f_low, b_top, b_low = moving
        to_f, to_b = terms_b[0], terms_f[0]
        f_low, b_top = two_sums((to_f[1], f_low), (to_b[0], b_top))
        f_low, b_top = forward(f_low), backward(b_top)
        f_top, b_low = two_sums((to_f[0], f_top), (to_b[1], b_low))
        f_top, b_low = forward(f_top), backward(b_low)
        grads = loss(units, fresh, other)
        plan = (
            (((0, 0), (1, 0), (3, 0), (5, 0)), 0, 0),
            (((0, cut), (2, 0), (4, 0), (6, 0)), 0, cut),
        )
        sources = [stream, *own, f_top, f_low, b_top, b_low]
        return *sums(plan, sources, cut, [stream.shape]), *grads

    def keep_stream(moving, units, fresh, other):
        return stream + jnp.concatenate(own), *loss(units, fresh, other)

    stream_out, grad_query, grad_pin = lax.cond(active, reduce_last, keep_stream, moving, units, fresh, other)
    return (stream_out[None], grad_query, grad_pin)


def solution(mesh):
    return jax.shard_map(
        local,
        mesh=mesh,
        in_specs=(
            P("section", "dp", None),
            P("section", None, None),
            P("section", None, None, "dp"),
            P("section", None, None, "dp"),
            P("section", None, "dp", None),
            P("section"),
            P("dp", None),
            P("dp", None),
            P("dp"),
        ),
        out_specs=(P("section", "dp", None), P("dp", "section"), P("dp", "section")),
        check_vma=False,
    )
```

profile of v0, /device:TPU:0, one launch (start us, length us, event | category | flops | bytes accessed | tf_op | source)
XLA Modules:
  0.0 210.1 jit_solution(3351198557398017616)
XLA Ops:
  1.3 136.0 %conditional.4 = (bf16[64,4096]{1,0:T(8,128)(2,1)}, bf16[64,4096]{1,0:T(8,128)(2,1)S(1)}, bf16[64,4096]{1,0:T(8,128)(2,1)}, bf16[64,4096]{1,0:T(8,128)(2,1)}, bf...) conditional(s32[]{:T(128)} %bitcast.16, (s32[]{:T(128)}, ...), branch_computations={%region_0.3_spmd, %region_3.7_spmd} | conditional | flops 19332341760 | bytes 97885880
  5.8 3.0 %collective-permute-start.22 = (bf16[64,4096]{1,0:T(8,128)(2,1)S(1)}, bf16[64,4096]{1,0:T(8,128)(2,1)S(1)}, u32[]{:S(2)}, u32[]{:S(2)}) collective-permute-start(bf16[64,4096]{1,0:T(8,128)(2,1)S(1)} %get-tuple-element.397.refs_1_), channel_id=1, source_target_pairs={{8,0},{16,8},{24,16},{28,24},{20,28},{12,20},{4,12},{0,4},{9,1},{1... | collective-permute-start | bytes 1572872 | tf_op jit(solution)/shard_map/cond/branch_1_fun/ppermute | solution.py:315
  17.0 6.9 %branch_1_fun.12 = (bf16[64,4096]{1,0:T(8,128)(2,1)}, bf16[64,4096]{1,0:T(8,128)(2,1)S(1)}, f32[8,4096]{1,0:T(8,128)S(1)}, bf16[4096,768]{1,0:T(8,128)(2,1)S(1)}...) custom-call(bf16[64,4096]{1,0:T(8,128)(2,1)S(1)} %get-tuple-element.398.refs_0_, ...), custom_call_target="tpu_custom_call" | custom-call | flops 2415919104 | bytes 2097152 | tf_op jit(solution)/shard_map/cond/branch_1_fun/pallas_call | solution.py:126
  24.0 9.5 %collective-permute-done.24 = s32[16,1]{0,1:T(1,128)S(1)} collective-permute-done((s32[16,1]{0,1:T(1,128)}, s32[16,1]{0,1:T(1,128)S(1)}, u32[]{:S(2)}, u32[]{:S(2)}) %collective-permute-start.24) | collective-permute-done | bytes 96 | tf_op jit(solution)/shard_map/cond/branch_1_fun/ppermute | solution.py:324
  33.9 3.9 %collective-permute-done.23 = bf16[2,16,1024]{2,1,0:T(8,128)(2,1)S(1)} collective-permute-done((bf16[2,16,1024]{2,1,0:T(8,128)(2,1)S(1)}, bf16[2,16,1024]{2,1,0:T(8,128)(2,1)S(1)}, u32[]{:S(2)}, u32[]{:S(2)}) %collective-permute-start.23) | collective-permute-done | bytes 65568 | tf_op jit(solution)/shard_map/cond/branch_1_fun/ppermute | solution.py:324
  42.0 6.6 %branch_1_fun.13 = (bf16[64,4096]{1,0:T(8,128)(2,1)}, bf16[64,4096]{1,0:T(8,128)(2,1)}, bf16[64,4096]{1,0:T(8,128)(2,1)}, bf16[64,4096]{1,0:T(8,128)(2,1)}, f32[8,4096]{1,0:T(8,128)S(1)}) custom-call(bf16[64,4096]{1,0:T(8,128)(2,1)S(1)} %collective-permute-done.19.refs_0_, bf16[64,4096]{1,0:T(8,128)(2,1)S(1)} %collective-permute-done.20.refs_1_, ...), custom_call_target="tpu_custom_call" | custom-call | flops 4831838208 | bytes 4194304 | tf_op jit(solution)/shard_map/cond/branch_1_fun/pallas_call | solution.py:137
  50.8 13.9 %collective-permute-done.29 = bf16[2,32,1024]{2,1,0:T(8,128)(2,1)S(1)} collective-permute-done((bf16[2,32,1024]{2,1,0:T(8,128)(2,1)S(1)}, bf16[2,32,1024]{2,1,0:T(8,128)(2,1)S(1)}, u32[]{:S(2)}, u32[]{:S(2)}) %collective-permute-start.29) | collective-permute-done | bytes 131104 | tf_op jit(solution)/shard_map/cond/branch_1_fun/ppermute | solution.py:324
  70.0 6.6 %branch_1_fun.14 = (bf16[64,4096]{1,0:T(8,128)(2,1)}, bf16[64,4096]{1,0:T(8,128)(2,1)}, bf16[64,4096]{1,0:T(8,128)(2,1)}, bf16[64,4096]{1,0:T(8,128)(2,1)}, f32[8,4096]{1,0:T(8,128)S(1)}) custom-call(bf16[64,4096]{1,0:T(8,128)(2,1)S(1)} %collective-permute-done.25.refs_0_, bf16[64,4096]{1,0:T(8,128)(2,1)S(1)} %collective-permute-done.26.refs_1_, ...), custom_call_target="tpu_custom_call" | custom-call | flops 4831838208 | bytes 4194304 | tf_op jit(solution)/shard_map/cond/branch_1_fun/pallas_call | solution.py:137
  79.2 6.5 %collective-permute-done.31.refs_0_ = bf16[64,4096]{1,0:T(8,128)(2,1)S(1)} collective-permute-done((bf16[64,4096]{1,0:T(8,128)(2,1)S(1)}, bf16[64,4096]{1,0:T(8,128)(2,1)S(1)}, u32[]{:S(2)}, u32[]{:S(2)}) %collective-permute-start.31) | collective-permute-done | bytes 524320 | tf_op jit(solution)/shard_map/cond/branch_1_fun/ppermute | solution.py:312
  86.4 4.6 %collective-permute-start.37 = (bf16[64,4096]{1,0:T(8,128)(2,1)S(1)}, bf16[64,4096]{1,0:T(8,128)(2,1)S(1)}, u32[]{:S(2)}, u32[]{:S(2)}) collective-permute-start(bf16[64,4096]{1,0:T(8,128)(2,1)S(1)} %collective-permute-done.31.refs_0_), channel_id=1, source_target_pairs={{0,8},{8,16},{16,24},{24,28},{28,20},{20,12},{12,4},{4,0},{1,9},{9... | collective-permute-start | bytes 1572872 | tf_op jit(solution)/shard_map/cond/branch_1_fun/ppermute | solution.py:312
  91.0 4.7 %collective-permute-done.32.refs_1_ = bf16[64,4096]{1,0:T(8,128)(2,1)S(1)} collective-permute-done((bf16[64,4096]{1,0:T(8,128)(2,1)S(1)}, bf16[64,4096]{1,0:T(8,128)(2,1)S(1)}, u32[]{:S(2)}, u32[]{:S(2)}) %collective-permute-start.32) | collective-permute-done | bytes 524320 | tf_op jit(solution)/shard_map/cond/branch_1_fun/ppermute | solution.py:312
  97.6 6.3 %branch_1_fun.15 = (bf16[64,4096]{1,0:T(8,128)(2,1)S(1)}, bf16[64,4096]{1,0:T(8,128)(2,1)}, bf16[64,4096]{1,0:T(8,128)(2,1)}, bf16[64,4096]{1,0:T(8,128)(2,1)S(1)}, f32[8,4096]{1,0:T(8,128)S(1)}) custom-call(bf16[64,4096]{1,0:T(8,128)(2,1)S(1)} %collective-permute-done.31.refs_0_, bf16[64,4096]{1,0:T(8,128)(2,1)S(1)} %collective-permute-done.32.refs_1_, ...), custom_call_target="tpu_custom_call" | custom-call | flops 4831838208 | bytes 4194304 | tf_op jit(solution)/shard_map/cond/branch_1_fun/pallas_call | solution.py:137
  103.9 4.7 %collective-permute-start.40 = (bf16[64,4096]{1,0:T(8,128)(2,1)S(1)}, bf16[64,4096]{1,0:T(8,128)(2,1)}, u32[]{:S(2)}, u32[]{:S(2)}) collective-permute-start(bf16[64,4096]{1,0:T(8,128)(2,1)S(1)} %get-tuple-element.203), channel_id=1, source_target_pairs={{0,8},{8,16},{16,24},{24,28},{28,20},{20,12},{12,4},{4,0},{1,9},{9... | collective-permute-start | bytes 1572872 | tf_op jit(solution)/shard_map/cond/branch_1_fun/ppermute | solution.py:312
  111.8 4.7 %collective-permute-done.40 = bf16[64,4096]{1,0:T(8,128)(2,1)} collective-permute-done((bf16[64,4096]{1,0:T(8,128)(2,1)S(1)}, bf16[64,4096]{1,0:T(8,128)(2,1)}, u32[]{:S(2)}, u32[]{:S(2)}) %collective-permute-start.40) | collective-permute-done | bytes 524320 | tf_op jit(solution)/shard_map/cond/branch_1_fun/ppermute | solution.py:312
  121.0 4.3 %collective-permute-start.39 = (bf16[64,4096]{1,0:T(8,128)(2,1)S(1)}, bf16[64,4096]{1,0:T(8,128)(2,1)}, u32[]{:S(2)}, u32[]{:S(2)}) collective-permute-start(bf16[64,4096]{1,0:T(8,128)(2,1)S(1)} %get-tuple-element.202), channel_id=1, source_target_pairs={{0,8},{8,16},{16,24},{24,28},{28,20},{20,12},{12,4},{4,0},{1,9},{9... | collective-permute-start | bytes 1572872 | tf_op jit(solution)/shard_map/cond/branch_1_fun/ppermute | solution.py:312
  128.0 7.0 %collective-permute-done.39 = bf16[64,4096]{1,0:T(8,128)(2,1)} collective-permute-done((bf16[64,4096]{1,0:T(8,128)(2,1)S(1)}, bf16[64,4096]{1,0:T(8,128)(2,1)}, u32[]{:S(2)}, u32[]{:S(2)}) %collective-permute-start.39) | collective-permute-done | bytes 524320 | tf_op jit(solution)/shard_map/cond/branch_1_fun/ppermute | solution.py:312
  138.4 35.6 %conditional.5 = ((bf16[64,4096]{1,0:T(8,128)(2,1)}, bf16[64,4096]{1,0:T(8,128)(2,1)}, bf16[64,4096]{1,0:T(8,128)(2,1)}, bf16[64,4096]{1,0:T(8,128)(2,1)})) conditional(s32[]{:T(128)} %bitcast.16, (bf16[64,4096]{1,0:T(8,128)(2,1)}, bf16[64,4096]{1,0:T(8,128)(2,1)}, bf16[64,4096]{1,0:T(8,128)(2,1)}, bf16[64,4096]{1,0:T(8,128)(2,1)}) %tuple.53, ...), branch_computations={%region_7.8_spmd, %region_8.9_spmd} | conditional | flops 3145728 | bytes 25166104 | solution.py:434
  146.0 9.1 %collective-permute-done.refs_1_ = bf16[64,4096]{1,0:T(8,128)(2,1)S(1)} collective-permute-done((bf16[64,4096]{1,0:T(8,128)(2,1)S(1)}, bf16[64,4096]{1,0:T(8,128)(2,1)S(1)}, u32[]{:S(2)}, u32[]{:S(2)}) %collective-permute-start) | collective-permute-done | bytes 524320 | tf_op jit(solution)/shard_map/cond/branch_1_fun/ppermute | solution.py:312
  158.8 7.5 %collective-permute-done.3 = bf16[64,4096]{1,0:T(8,128)(2,1)} collective-permute-done((bf16[64,4096]{1,0:T(8,128)(2,1)S(1)}, bf16[64,4096]{1,0:T(8,128)(2,1)}, u32[]{:S(2)}, u32[]{:S(2)}) %collective-permute-start.3) | collective-permute-done | bytes 524320 | tf_op jit(solution)/shard_map/cond/branch_1_fun/ppermute | solution.py:312
  166.7 7.0 %collective-permute-done.2 = bf16[64,4096]{1,0:T(8,128)(2,1)} collective-permute-done((bf16[64,4096]{1,0:T(8,128)(2,1)S(1)}, bf16[64,4096]{1,0:T(8,128)(2,1)}, u32[]{:S(2)}, u32[]{:S(2)}) %collective-permute-start.2) | collective-permute-done | bytes 524320 | tf_op jit(solution)/shard_map/cond/branch_1_fun/ppermute | solution.py:312
  179.0 30.9 %conditional.6 = (f32[16,1024]{1,0:T(8,128)}, f32[16,1024]{1,0:T(8,128)}, bf16[1,128,4096]{2,1,0:T(8,128)(2,1)}) conditional(s32[]{:T(128)} %bitcast.16, (s32[2]{0:T(128)S(1)}, bf16[256,1024]{1,0:T(8,128)(2,1)S(1)}, bf16[256,1024]{1,0:T(8,128)(2,1)S(1)}, bf16[544,1024]{1,0:T(8,128)(2,1)S(1)}, bf16[32,1024]{1,0:T(8,128)(2,1)S(1)}, ...), branch_computations={%region_9.10_spmd, %region_10.11_spmd} | conditional | flops 4194304 | bytes 46400892 | solution.py:474
  188.8 4.2 %branch_1_fun.20 = (f32[16,1024]{1,0:T(8,128)}, f32[16,1024]{1,0:T(8,128)}) custom-call(s32[2]{0:T(128)S(1)} %get-tuple-element.243.where_ref, bf16[256,1024]{1,0:T(8,128)(2,1)} %copy-done.6, bf16[256,1024]{1,0:T(8,128)(2,1)} %copy-done.7, bf16[544,1024]{1,0:T(8,128)(2,1)} %copy-done, bf16[32,1024]{1,0:T(8,128)(2,1)S(1)} %get-tuple-element.247.refs_3_, ...), custom_call_target="tpu_custom_call" | custom-call | tf_op jit(solution)/shard_map/cond/branch_1_fun/pallas_call | solution.py:448
  193.0 3.9 %collective-permute-done.7.refs_4_ = bf16[64,4096]{1,0:T(8,128)(2,1)S(1)} collective-permute-done((bf16[64,4096]{1,0:T(8,128)(2,1)S(1)}, bf16[64,4096]{1,0:T(8,128)(2,1)S(1)}, u32[]{:S(2)}, u32[]{:S(2)}) %collective-permute-start.7) | collective-permute-done | bytes 524320 | tf_op jit(solution)/shard_map/cond/branch_1_fun/ppermute | solution.py:312
  197.5 9.9 %collective-permute-done.6.refs_3_ = bf16[64,4096]{1,0:T(8,128)(2,1)S(1)} collective-permute-done((bf16[64,4096]{1,0:T(8,128)(2,1)}, bf16[64,4096]{1,0:T(8,128)(2,1)S(1)}, u32[]{:S(2)}, u32[]{:S(2)}) %collective-permute-start.6) | collective-permute-done | bytes 524320 | tf_op jit(solution)/shard_map/cond/branch_1_fun/ppermute | solution.py:312
  (145 shorter events, 73.2 us)
Async XLA Ops:
  5.8 32.0 %collective-permute-start.22 = (bf16[64,4096]{1,0:T(8,128)(2,1)S(1)}, bf16[64,4096]{1,0:T(8,128)(2,1)S(1)}, u32[]{:S(2)}, u32[]{:S(2)}) collective-permute-start(bf16[64,4096]{1,0:T(8,128)(2,1)S(1)} %get-tuple-element.397.refs_1_), channel_id=1, source_target_pairs={{8,0},{16,8},{24,16},{28,24},{20,28},{12,20},{4,12},{0,4},{9,1},{1... | collective-permute-start | bytes 1572872 | tf_op jit(solution)/shard_map/cond/branch_1_fun/ppermute | solution.py:315
  8.8 29.0 %collective-permute-start.20 = (bf16[64,4096]{1,0:T(8,128)(2,1)S(1)}, bf16[64,4096]{1,0:T(8,128)(2,1)S(1)}, u32[]{:S(2)}, u32[]{:S(2)}) collective-permute-start(bf16[64,4096]{1,0:T(8,128)(2,1)S(1)} %get-tuple-element.397.refs_1_), channel_id=1, source_target_pairs={{0,8},{8,16},{16,24},{24,28},{28,20},{20,12},{12,4},{4,0},{1,9},{9... | collective-permute-start | bytes 1572872 | tf_op jit(solution)/shard_map/cond/branch_1_fun/ppermute | solution.py:312
  8.9 28.9 %collective-permute-start.21 = (bf16[64,4096]{1,0:T(8,128)(2,1)S(1)}, bf16[64,4096]{1,0:T(8,128)(2,1)S(1)}, u32[]{:S(2)}, u32[]{:S(2)}) collective-permute-start(bf16[64,4096]{1,0:T(8,128)(2,1)S(1)} %get-tuple-element.398.refs_0_), channel_id=1, source_target_pairs={{8,0},{16,8},{24,16},{28,24},{20,28},{12,20},{4,12},{0,4},{9,1},{1... | collective-permute-start | bytes 1572872 | tf_op jit(solution)/shard_map/cond/branch_1_fun/ppermute | solution.py:315
  10.8 27.0 %collective-permute-start.19 = (bf16[64,4096]{1,0:T(8,128)(2,1)S(1)}, bf16[64,4096]{1,0:T(8,128)(2,1)S(1)}, u32[]{:S(2)}, u32[]{:S(2)}) collective-permute-start(bf16[64,4096]{1,0:T(8,128)(2,1)S(1)} %get-tuple-element.398.refs_0_), channel_id=1, source_target_pairs={{0,8},{8,16},{16,24},{24,28},{28,20},{20,12},{12,4},{4,0},{1,9},{9... | collective-permute-start | bytes 1572872 | tf_op jit(solution)/shard_map/cond/branch_1_fun/ppermute | solution.py:312
  11.0 22.5 %collective-permute-start.24 = (s32[16,1]{0,1:T(1,128)}, s32[16,1]{0,1:T(1,128)S(1)}, u32[]{:S(2)}, u32[]{:S(2)}) collective-permute-start(s32[16,1]{0,1:T(1,128)} %bitcast.44), channel_id=1, source_target_pairs={{0,4},{4,0},{8,12},{12,8},{16,20},{20,16},{24,28},{28,24},{1,5},{5... | collective-permute-start | bytes 200 | tf_op jit(solution)/shard_map/cond/branch_1_fun/ppermute | solution.py:324
  37.9 26.8 %collective-permute-start.25 = (bf16[64,4096]{1,0:T(8,128)(2,1)S(1)}, bf16[64,4096]{1,0:T(8,128)(2,1)S(1)}, u32[]{:S(2)}, u32[]{:S(2)}) collective-permute-start(bf16[64,4096]{1,0:T(8,128)(2,1)S(1)} %collective-permute-done.19.refs_0_), channel_id=1, source_target_pairs={{0,8},{8,16},{16,24},{24,28},{28,20},{20,12},{12,4},{4,0},{1,9},{9... | collective-permute-start | bytes 1572872 | tf_op jit(solution)/shard_map/cond/branch_1_fun/ppermute | solution.py:312
  39.9 24.8 %collective-permute-start.28 = (bf16[64,4096]{1,0:T(8,128)(2,1)S(1)}, bf16[64,4096]{1,0:T(8,128)(2,1)S(1)}, u32[]{:S(2)}, u32[]{:S(2)}) collective-permute-start(bf16[64,4096]{1,0:T(8,128)(2,1)S(1)} %collective-permute-done.22.refs_3_), channel_id=1, source_target_pairs={{8,0},{16,8},{24,16},{28,24},{20,28},{12,20},{4,12},{0,4},{9,1},{1... | collective-permute-start | bytes 1572872 | tf_op jit(solution)/shard_map/cond/branch_1_fun/ppermute | solution.py:315
  40.0 24.8 %collective-permute-start.26 = (bf16[64,4096]{1,0:T(8,128)(2,1)S(1)}, bf16[64,4096]{1,0:T(8,128)(2,1)S(1)}, u32[]{:S(2)}, u32[]{:S(2)}) collective-permute-start(bf16[64,4096]{1,0:T(8,128)(2,1)S(1)} %collective-permute-done.20.refs_1_), channel_id=1, source_target_pairs={{0,8},{8,16},{16,24},{24,28},{28,20},{20,12},{12,4},{4,0},{1,9},{9... | collective-permute-start | bytes 1572872 | tf_op jit(solution)/shard_map/cond/branch_1_fun/ppermute | solution.py:312
  41.9 22.8 %collective-permute-start.27 = (bf16[64,4096]{1,0:T(8,128)(2,1)S(1)}, bf16[64,4096]{1,0:T(8,128)(2,1)S(1)}, u32[]{:S(2)}, u32[]{:S(2)}) collective-permute-start(bf16[64,4096]{1,0:T(8,128)(2,1)S(1)} %collective-permute-done.21.refs_2_), channel_id=1, source_target_pairs={{8,0},{16,8},{24,16},{28,24},{20,28},{12,20},{4,12},{0,4},{9,1},{1... | collective-permute-start | bytes 1572872 | tf_op jit(solution)/shard_map/cond/branch_1_fun/ppermute | solution.py:315
  48.7 16.0 %collective-permute-start.29 = (bf16[2,32,1024]{2,1,0:T(8,128)(2,1)S(1)}, bf16[2,32,1024]{2,1,0:T(8,128)(2,1)S(1)}, u32[]{:S(2)}, u32[]{:S(2)}) collective-permute-start(bf16[2,32,1024]{2,1,0:T(8,128)(2,1)S(1)} %pad_maximum_fusion.4), channel_id=1, source_target_pairs={{0,8},{4,12},{8,0},{12,4},{16,24},{20,28},{24,16},{28,20},{1,9},{5... | collective-permute-start | bytes 393224 | tf_op jit(solution)/shard_map/cond/branch_1_fun/ppermute | solution.py:324
  67.7 18.0 %collective-permute-start.31 = (bf16[64,4096]{1,0:T(8,128)(2,1)S(1)}, bf16[64,4096]{1,0:T(8,128)(2,1)S(1)}, u32[]{:S(2)}, u32[]{:S(2)}) collective-permute-start(bf16[64,4096]{1,0:T(8,128)(2,1)S(1)} %collective-permute-done.25.refs_0_), channel_id=1, source_target_pairs={{0,8},{8,16},{16,24},{24,28},{28,20},{20,12},{12,4},{4,0},{1,9},{9... | collective-permute-start | bytes 1572872 | tf_op jit(solution)/shard_map/cond/branch_1_fun/ppermute | solution.py:312
  68.0 18.4 %collective-permute-start.34 = (bf16[64,4096]{1,0:T(8,128)(2,1)S(1)}, bf16[64,4096]{1,0:T(8,128)(2,1)S(1)}, u32[]{:S(2)}, u32[]{:S(2)}) collective-permute-start(bf16[64,4096]{1,0:T(8,128)(2,1)S(1)} %collective-permute-done.28.refs_3_), channel_id=1, source_target_pairs={{8,0},{16,8},{24,16},{28,24},{20,28},{12,20},{4,12},{0,4},{9,1},{1... | collective-permute-start | bytes 1572872 | tf_op jit(solution)/shard_map/cond/branch_1_fun/ppermute | solution.py:315
  69.8 25.9 %collective-permute-start.32 = (bf16[64,4096]{1,0:T(8,128)(2,1)S(1)}, bf16[64,4096]{1,0:T(8,128)(2,1)S(1)}, u32[]{:S(2)}, u32[]{:S(2)}) collective-permute-start(bf16[64,4096]{1,0:T(8,128)(2,1)S(1)} %collective-permute-done.26.refs_1_), channel_id=1, source_target_pairs={{0,8},{8,16},{16,24},{24,28},{28,20},{20,12},{12,4},{4,0},{1,9},{9... | collective-permute-start | bytes 1572872 | tf_op jit(solution)/shard_map/cond/branch_1_fun/ppermute | solution.py:312
  76.6 21.0 %collective-permute-start.33 = (bf16[64,4096]{1,0:T(8,128)(2,1)S(1)}, bf16[64,4096]{1,0:T(8,128)(2,1)S(1)}, u32[]{:S(2)}, u32[]{:S(2)}) collective-permute-start(bf16[64,4096]{1,0:T(8,128)(2,1)S(1)} %collective-permute-done.27.refs_2_), channel_id=1, source_target_pairs={{8,0},{16,8},{24,16},{28,24},{20,28},{12,20},{4,12},{0,4},{9,1},{1... | collective-permute-start | bytes 1572872 | tf_op jit(solution)/shard_map/cond/branch_1_fun/ppermute | solution.py:315
  86.4 22.3 %collective-permute-start.37 = (bf16[64,4096]{1,0:T(8,128)(2,1)S(1)}, bf16[64,4096]{1,0:T(8,128)(2,1)S(1)}, u32[]{:S(2)}, u32[]{:S(2)}) collective-permute-start(bf16[64,4096]{1,0:T(8,128)(2,1)S(1)} %collective-permute-done.31.refs_0_), channel_id=1, source_target_pairs={{0,8},{8,16},{16,24},{24,28},{28,20},{20,12},{12,4},{4,0},{1,9},{9... | collective-permute-start | bytes 1572872 | tf_op jit(solution)/shard_map/cond/branch_1_fun/ppermute | solution.py:312
  91.0 17.6 %collective-permute-start.38 = (bf16[64,4096]{1,0:T(8,128)(2,1)S(1)}, bf16[64,4096]{1,0:T(8,128)(2,1)S(1)}, u32[]{:S(2)}, u32[]{:S(2)}) collective-permute-start(bf16[64,4096]{1,0:T(8,128)(2,1)S(1)} %collective-permute-done.34.refs_3_), channel_id=1, source_target_pairs={{8,0},{16,8},{24,16},{28,24},{20,28},{12,20},{4,12},{0,4},{9,1},{1... | collective-permute-start | bytes 1572872 | tf_op jit(solution)/shard_map/cond/branch_1_fun/ppermute | solution.py:315
  138.4 35.6 %collective-permute-start.46 = (bf16[288,1024]{1,0:T(8,128)(2,1)}, bf16[288,1024]{1,0:T(8,128)(2,1)}, u32[]{:S(2)}, u32[]{:S(2)}) collective-permute-start(bf16[288,1024]{1,0:T(8,128)(2,1)} %pad_maximum_fusion.7), channel_id=1, source_target_pairs={{0,2},{1,3},{2,0},{3,1},{4,6},{5,7},{6,4},{7,5},{8,10},{9,11},{10,... | collective-permute-start | bytes 1769480 | tf_op jit(solution)/shard_map/ppermute | solution.py:417
  140.1 14.9 %collective-permute-start = (bf16[64,4096]{1,0:T(8,128)(2,1)S(1)}, bf16[64,4096]{1,0:T(8,128)(2,1)S(1)}, u32[]{:S(2)}, u32[]{:S(2)}) collective-permute-start(bf16[64,4096]{1,0:T(8,128)(2,1)S(1)} %get-tuple-element.219), channel_id=1, source_target_pairs={{0,8},{8,16},{16,24},{24,28},{28,20},{20,12},{12,4},{4,0},{1,9},{9... | collective-permute-start | bytes 1572872 | tf_op jit(solution)/shard_map/cond/branch_1_fun/ppermute | solution.py:312
  143.9 22.5 %collective-permute-start.3 = (bf16[64,4096]{1,0:T(8,128)(2,1)S(1)}, bf16[64,4096]{1,0:T(8,128)(2,1)}, u32[]{:S(2)}, u32[]{:S(2)}) collective-permute-start(bf16[64,4096]{1,0:T(8,128)(2,1)S(1)} %get-tuple-element.227), channel_id=1, source_target_pairs={{0,8},{8,16},{16,24},{24,28},{28,20},{20,12},{12,4},{4,0},{1,9},{9... | collective-permute-start | bytes 1572872 | tf_op jit(solution)/shard_map/cond/branch_1_fun/ppermute | solution.py:312
  144.3 22.4 %collective-permute-start.4 = (bf16[64,4096]{1,0:T(8,128)(2,1)S(1)}, bf16[64,4096]{1,0:T(8,128)(2,1)}, u32[]{:S(2)}, u32[]{:S(2)}) collective-permute-start(bf16[64,4096]{1,0:T(8,128)(2,1)S(1)} %get-tuple-element.228), channel_id=1, source_target_pairs={{8,0},{16,8},{24,16},{28,24},{20,28},{12,20},{4,12},{0,4},{9,1},{1... | collective-permute-start | bytes 1572872 | tf_op jit(solution)/shard_map/cond/branch_1_fun/ppermute | solution.py:315
  156.8 16.9 %collective-permute-start.2 = (bf16[64,4096]{1,0:T(8,128)(2,1)S(1)}, bf16[64,4096]{1,0:T(8,128)(2,1)}, u32[]{:S(2)}, u32[]{:S(2)}) collective-permute-start(bf16[64,4096]{1,0:T(8,128)(2,1)S(1)} %get-tuple-element.222), channel_id=1, source_target_pairs={{0,8},{8,16},{16,24},{24,28},{28,20},{20,12},{12,4},{4,0},{1,9},{9... | collective-permute-start | bytes 1572872 | tf_op jit(solution)/shard_map/cond/branch_1_fun/ppermute | solution.py:312
  157.0 17.0 %collective-permute-start.5 = (bf16[64,4096]{1,0:T(8,128)(2,1)S(1)}, bf16[64,4096]{1,0:T(8,128)(2,1)}, u32[]{:S(2)}, u32[]{:S(2)}) collective-permute-start(bf16[64,4096]{1,0:T(8,128)(2,1)S(1)} %get-tuple-element.229), channel_id=1, source_target_pairs={{8,0},{16,8},{24,16},{28,24},{20,28},{12,20},{4,12},{0,4},{9,1},{1... | collective-permute-start | bytes 1572872 | tf_op jit(solution)/shard_map/cond/branch_1_fun/ppermute | solution.py:315
  186.6 20.8 %collective-permute-start.6 = (bf16[64,4096]{1,0:T(8,128)(2,1)}, bf16[64,4096]{1,0:T(8,128)(2,1)S(1)}, u32[]{:S(2)}, u32[]{:S(2)}) collective-permute-start(bf16[64,4096]{1,0:T(8,128)(2,1)} %get-tuple-element.260), channel_id=1, source_target_pairs={{0,8},{8,16},{16,24},{24,28},{28,20},{20,12},{12,4},{4,0},{1,9},{9... | collective-permute-start | bytes 1572872 | tf_op jit(solution)/shard_map/cond/branch_1_fun/ppermute | solution.py:312
  187.1 20.4 %collective-permute-start.9 = (bf16[64,4096]{1,0:T(8,128)(2,1)}, bf16[64,4096]{1,0:T(8,128)(2,1)S(1)}, u32[]{:S(2)}, u32[]{:S(2)}) collective-permute-start(bf16[64,4096]{1,0:T(8,128)(2,1)} %get-tuple-element.267), channel_id=1, source_target_pairs={{8,0},{16,8},{24,16},{28,24},{20,28},{12,20},{4,12},{0,4},{9,1},{1... | collective-permute-start | bytes 1572872 | tf_op jit(solution)/shard_map/cond/branch_1_fun/ppermute | solution.py:315
  (31 other events, 311.4 us)
where the time goes:
time: 211 us; the launch traced here: 210 us
  waiting for transfers between devices  99.8 us (47%)
  starting transfers between devices  46.7 us (22%)
  Pallas kernels  44.8 us (21%)
  other arithmetic  11.5 us (5%)
  local copies, waits for them, and re-layouts  5.27 us (2%)
    ppermute x14, waiting for transfers between devices, forward(): return lax.ppermute(values, 'dp', ring)  60.2 us
    ppermute x6, waiting for transfers between devices, doubled(): lax.ppermute(values, 'dp', [(i, i ^ reach) for i in range(replicas)])  27.9 us
    pallas_call x4, Pallas kernels, multiply(): pl.pallas_call(functools.partial(next_kernel, count), out_shape=out_shape...  22.4 us
    ppermute x14, starting transfers between devices, forward(): return lax.ppermute(values, 'dp', ring)  20.5 us
    ppermute x14, starting transfers between devices, backward(): return lax.ppermute(values, 'dp', ring_back)  16.9 us
    pallas_call x6, Pallas kernels, sums(): pl.pallas_call(functools.partial(sum_kernel, plan, len(sources)), out_sha...  11.2 us
    ppermute x14, waiting for transfers between devices, backward(): return lax.ppermute(values, 'dp', ring_back)  8.95 us
    ppermute x6, starting transfers between devices, doubled(): lax.ppermute(values, 'dp', [(i, i ^ reach) for i in range(replicas)])  7.27 us
  transfers between devices with their start and end apart: 39, of which 23 were waited for; matrix products, arithmetic and copies ran while one was open for 4% of the time, Pallas kernels for 19%

commit v1 on v0

--- a/solution.py
+++ b/solution.py
@@ -16,12 +16,6 @@
 
 def ring_order(size):
     return list(range(0, size, 2)) + list(range(size - 1, 0, -2))
-
-
-def rms_scaled(stream, gain_row):
-    values = stream.astype(jnp.float32)
-    factor = lax.rsqrt(jnp.mean(values * values, axis=-1, keepdims=True) + EPSILON)
-    return (values * factor * gain_row.astype(jnp.float32)).astype(jnp.bfloat16)
 
 
 def unit_rows(values):
@@ -146,6 +140,50 @@
     return outs[:count], outs[count]
 
 
+def norm_kernel(parts, stream, gain, top, low, loaded, result, in_sems, out_sems):
+    rows = stream.shape[0] // parts
+    loads = []
+    for i in range(parts):
+        here = pl.ds(i * rows, rows)
+        loads.append(pltpu.make_async_copy(stream.at[here], loaded.at[here], in_sems.at[i]))
+        loads[-1].start()
+    scale = gain[...].astype(jnp.float32)
+    stores = []
+    for i in range(parts):
+        loads[i].wait()
+        values = loaded[i * rows : (i + 1) * rows].astype(jnp.float32)
+        mean = jnp.mean(values * values, axis=1, keepdims=True)
+        values = values * lax.rsqrt(mean + EPSILON) * scale
+        result[i * rows : (i + 1) * rows] = values.astype(jnp.bfloat16)
+        out, row = (top, i * rows) if i < parts // 2 else (low, (i - parts // 2) * rows)
+        store = pltpu.make_async_copy(
+            result.at[pl.ds(i * rows, rows)], out.at[pl.ds(row, rows)], out_sems.at[i]
+        )
+        store.start()
+        stores.append(store)
+    for store in stores:
+        store.wait()
+
+
+def normalized(stream, gain):
+    rows, width = stream.shape
+    parts = 4
+    out = jax.ShapeDtypeStruct((rows // 2, width), jnp.bfloat16)
+    return pl.pallas_call(
+        functools.partial(norm_kernel, parts),
+        out_shape=[out, out],
+        in_specs=[ANYWHERE, IN_VMEM],
+        out_specs=[ANYWHERE] * 2,
+        scratch_shapes=[
+            pltpu.VMEM((rows, width), jnp.bfloat16),
+            pltpu.VMEM((rows, width), jnp.bfloat16),
+            pltpu.SemaphoreType.DMA((parts,)),
+            pltpu.SemaphoreType.DMA((parts,)),
+        ],
+        compiler_params=pltpu.CompilerParams(vmem_limit_bytes=16 << 20),
+    )(stream, gain)
+
+
 def sum_kernel(plan, sources, *refs):
     ins, outs, (loaded, result, in_sems, out_sems) = refs[:sources], refs[sources:-4], refs[-4:]
     rows = result.shape[1]
@@ -187,12 +225,12 @@
         store.wait()
 
 
-def sums(plan, sources, rows, out_shapes):
+def sums(plan, sources, rows, out_shapes, kind=jax.ShapeDtypeStruct):
     terms = sum(len(entry[0]) for entry in plan)
     width = sources[0].shape[1]
     return pl.pallas_call(
         functools.partial(sum_kernel, plan, len(sources)),
-        out_shape=[jax.ShapeDtypeStruct(shape, jnp.bfloat16) for shape in out_shapes],
+        out_shape=[kind(shape, jnp.bfloat16) for shape in out_shapes],
         in_specs=[ANYWHERE] * len(sources),
         out_specs=[ANYWHERE] * len(out_shapes),
         scratch_shapes=[
@@ -214,9 +252,34 @@
     return sums(plan, [*first, *second], shape[0], [shape, shape])
 
 
+def rows_kernel(slots, position, stream, *refs):
+    tails, out = refs[:-1], refs[-1]
+    for offset, (source, slot) in enumerate(slots):
+        row = tails[source][slot : slot + 1]
+        if offset == 0:
+            row = row + stream[...].astype(jnp.float32)[15:]
+        out[pl.ds(lax.rem(position[0] + offset, len(slots)), 1)] = row
+
+
+def ring_rows(slots, tails, position, stream):
+    width = stream.shape[1]
+    last_block = stream.shape[0] // 16 - 1
+    shape = (len(slots), width)
+    return pl.pallas_call(
+        functools.partial(rows_kernel, slots),
+        grid=(1,),
+        out_shape=jax.ShapeDtypeStruct(shape, jnp.float32),
+        in_specs=[
+            pl.BlockSpec(memory_space=pltpu.SMEM),
+            pl.BlockSpec((16, width), lambda i: (last_block, 0)),
+        ]
+        + [pl.BlockSpec((8, width), lambda i: (0, 0))] * len(tails),
+        out_specs=pl.BlockSpec(shape, lambda i: (0, 0)),
+    )(position, stream, *tails)
+
+
 def loss_kernel(offsets, replicas, pair_dev, where_ref, *refs):
-    unit_refs, refs = refs[:-7], refs[-7:]
-    fresh_ref, other_ref, target_ref, query_ref, pin_ref, grad_query, grad_pin = refs
+    known, (query_ref, pin_ref, grad_query, grad_pin) = refs[:-4], refs[-4:]
     me, section = where_ref[0], where_ref[1]
     sections = len(offsets)
     width = grad_query.shape[1]
@@ -225,14 +288,15 @@
     def numbers(shape, dim):
         return lax.broadcasted_iota(jnp.int32, shape, dim)
 
-    units = []
-    for ref in unit_refs:
-        count = ref.shape[0] // (2 * pairs)
-        units += [ref.at[pl.ds(2 * pairs * i, 2 * pairs)] for i in range(count)]
-
-    fresh = fresh_ref[...] + other_ref[other_ref.shape[0] - fresh_ref.shape[0] :]
+    size = 2 * pairs + sections * replicas
+    units = [
+        ref.at[pl.ds(size * i, size)] for ref in known for i in range(ref.shape[0] // size)
+    ]
+
+    fresh = sum(unit[2 * pairs :].astype(jnp.float32) for unit in units).astype(jnp.bfloat16)
     row = numbers((sections * replicas, 1), 0)
-    source = (me ^ (row % replicas)) * sections
+    replica = me ^ (row % replicas)
+    source = jnp.where(replica % 2 == 0, replica // 2, replicas - (replica + 1) // 2) * sections
     for j, offset in enumerate(offsets):
         source = source + jnp.where(row // replicas == j, section ^ offset, 0)
     pick = (source == numbers((1, sections * replicas), 1)).astype(jnp.float32)
@@ -249,7 +313,7 @@
     for j in range(sections):
         unit = fresh[j * replicas : (j + 1) * replicas] / fresh_length
         placed = jnp.dot(spread, unit.astype(jnp.bfloat16), preferred_element_type=jnp.float32)
-        pins = jnp.where(first, placed, units[j][pairs:].astype(jnp.float32)).astype(jnp.bfloat16)
+        pins = jnp.where(first, placed, units[j][pairs : 2 * pairs].astype(jnp.float32)).astype(jnp.bfloat16)
         if j == 0:
             own_unit, own_pins = unit[:1], pins
         cosines = cosines + lax.dot_general(
@@ -259,7 +323,13 @@
     probs = raised / jnp.sum(raised, axis=1, keepdims=True)
     column = numbers((1, pairs), 1)
     pin_number = (me ^ (column // pair_dev)) * pair_dev + column % pair_dev
-    onehot = (pin_number == target_ref[...]).astype(jnp.float32)
+    ahead = (pair // pair_dev * pair_dev == column).astype(jnp.float32).astype(jnp.bfloat16)
+    targets = jnp.dot(
+        ahead, units[0][pairs : 2 * pairs, :128], preferred_element_type=jnp.float32
+    )
+    is_own = pair % pair_dev == numbers((1, 128), 1)
+    target = jnp.sum(jnp.where(is_own, targets, 0.0), axis=1, keepdims=True)
+    onehot = (pin_number.astype(jnp.float32) == target).astype(jnp.float32)
     weights = ((probs - onehot) * INV_TEMP).astype(jnp.bfloat16)
     floats = weights.astype(jnp.float32)
     dots = floats * cosines
@@ -294,19 +364,18 @@
     half = replicas // 2
     cut = rows_dev // 2
     order = ring_order(replicas)
-    place = [order.index(replica) for replica in range(replicas)]
     ring = [(order[i], order[(i + 1) % replicas]) for i in range(replicas)]
     ring_back = [(b, a) for a, b in ring]
     me = lax.axis_index("dp")
     section = lax.axis_index("section")
     position = jnp.where(me % 2 == 0, me // 2, replicas - (me + 1) // 2)
-    turn = (replicas - position).astype(jnp.uint32)
+    position = position.reshape(1)
     last = sections - 1
     active = layer_counts[0] > 0
     stream = held[0]
     col_width = model_width // sections
     col_start = (section * col_width).astype(jnp.uint32)
-    turn, position, col_start = lax.optimization_barrier((turn, position, col_start))
+    position, col_start = lax.optimization_barrier((position, col_start))
 
     def forward(values):
         return lax.ppermute(values, "dp", ring)
@@ -321,8 +390,8 @@
         return lax.optimization_barrier((values, others))[0]
 
     def doubled(values, reach):
-        others = lax.ppermute(values, "dp", [(i, i ^ reach) for i in range(replicas)])
-        return tuple(jnp.concatenate([v, o], axis=v.ndim - 2) for v, o in zip(values, others))
+        other = lax.ppermute(values, "dp", [(i, i ^ reach) for i in range(replicas)])
+        return jnp.concatenate([values, other], axis=1)
 
     def gathered(values, reach):
         while reach < replicas:
@@ -338,58 +407,70 @@
             reach *= 2
         return values
 
-    def with_held(rows):
-        rows = jnp.concatenate([rows, rows])
-        rows = lax.dynamic_slice(rows, (turn, jnp.uint32(0)), (replicas, model_width))
-        mine = jnp.arange(replicas)[:, None] == position
-        return rows + jnp.where(mine, stream[rows_dev - 1 :].astype(jnp.float32), 0.0)
-
-    def unit_columns():
+    def unit_columns(query_bank, pin_bank):
         query_send = unit_rows(query_bank)[0].astype(jnp.bfloat16)
-        pin_send = unit_rows(pin_bank)[0].astype(jnp.bfloat16)
-        return jnp.stack([own_columns(query_send), own_columns(pin_send)]), positive[:, None]
+        pin_send = own_columns(unit_rows(pin_bank)[0].astype(jnp.bfloat16))
+        numbers = jnp.pad(positive, (0, col_width - pair_dev)).astype(jnp.bfloat16)
+        is_first = (jnp.arange(pair_dev) == 0)[:, None]
+        return jnp.stack([own_columns(query_send), jnp.where(is_first, numbers, pin_send)])
 
     def gather_and_multiply():
-        normed = rms_scaled(stream, norm_gain[0])
-        f_top, f_low = normed[:cut], normed[cut:]
+        f_top, f_low = normalized(stream, norm_gain[0])
         b_top, b_low = f_top, f_low
+        first = [f_top, f_low]
         f_top, b_low = forward(f_top), backward(b_low)
         f_low, b_top = forward(f_low), backward(b_top)
         own, tails, weights = multiply(
-            [normed[:cut], normed[cut:]], [w_gate[0, 0], w_up[0, 0], w_down[0, 0]], True
-        )
-        sends = doubled(unit_columns(), 1)
-        reach = 2
-        ready = (own, sends)
-        terms_f, terms_b, rows_f, rows_b = [], [], [], [tails[1:2]]
+            first, [w_gate[0, 0], w_up[0, 0], w_down[0, 0]], True
+        )
+        sends = unit_columns(*after((query_bank, pin_bank), own))
+        reach = 1
+        ready_near, ready_far = own, own
+        terms_f, terms_b, all_tails = [], [], [tails]
         for step in range(1, half):
-            arrived = [f_top, f_low, b_top, b_low]
-            f_top, b_low = after((f_top, b_low), ready)
+            near, rest = (f_top, b_low), (f_low, b_top)
+            f_top, b_low = after(near, ready_near)
             f_top, b_low = forward(f_top), backward(b_low)
+            (tf_top, tb_low), near_tails = multiply(near, weights, False)
+            ready_far = (tf_top, tb_low, ready_far)
             if step < half - 1:
-                f_low, b_top = after((f_low, b_top), ready)
+                f_low, b_top = after(rest, ready_far)
                 f_low, b_top = forward(f_low), backward(b_top)
+            else:
+                tf_send, tb_send = after((tf_top, tb_low), ready_far)
+                f_low, b_top = forward(tb_send), backward(tf_send)
             if reach < replicas:
-                sends = doubled(after(sends, arrived), reach)
+                sends = doubled(after(sends, near), reach)
                 reach *= 2
-            terms, tails = multiply(arrived, weights, False)
-            terms_f.append(terms[:2])
-            terms_b.append(terms[2:])
-            rows_f.append(tails[1:2])
-            rows_b.append(tails[3:4])
-            ready = (terms, sends)
+            ready_far = sends
+            (tf_low, tb_top), rest_tails = multiply(rest, weights, False)
+            ready_near = (tf_low, tb_top)
+            terms_f.append((tf_top, tf_low))
+            terms_b.append((tb_top, tb_low))
+            all_tails += [near_tails, rest_tails]
         sends = gathered(sends, reach)
-        f_low, b_top = forward(terms_b[-1][1]), backward(terms_f[-1][0])
         far, tails = multiply([f_top, b_low], weights, False)
         f_top, b_low = forward(far[0]), backward(far[1])
-        rows = jnp.concatenate(rows_b + [tails[1:2]] + rows_f[::-1])
-        rows = after(rows, (f_low, b_top))
-        fresh = added_up(with_held(rows)).astype(jnp.bfloat16)
+        (f_top, b_low), sends = lax.optimization_barrier(((f_top, b_low), sends))
+        f_top, b_low = two_sums((terms_b[-1][0], f_top), (terms_f[-1][1], b_low))
+        all_tails.append(tails)
+        slots = (
+            [(0, 1)]
+            + [(2 * step - 1, 1) for step in range(1, half)]
+            + [(2 * half - 1, 1)]
+            + [(2 * step, 0) for step in range(half - 1, 0, -1)]
+        )
+        all_tails = after(all_tails, (f_top, b_low))
+        f_top, b_low = forward(f_top), backward(b_low)
+        rows = ring_rows(slots, all_tails, position, stream)
+        fresh = added_up(rows).astype(jnp.bfloat16)
         moving = (f_top, f_low, b_top, b_low)
         return tuple(own), tuple(terms_f), tuple(terms_b), moving, fresh, sends
 
     def gather_only():
-        fresh = added_up(with_held(jnp.zeros((replicas, model_width), jnp.float32)))
+        fresh = added_up(
+            ring_rows([(0, 0)] * replicas, [jnp.zeros((8, model_width), jnp.float32)], position, stream)
+        )
         empty = jnp.zeros((cut, model_width), jnp.bfloat16)
         some = tuple((empty, empty) for _ in range(1, half))
         return (
@@ -398,80 +479,74 @@
             some,
             (empty,) * 4,
             fresh.astype(jnp.bfloat16),
-            gathered(unit_columns(), 1),
+            gathered(unit_columns(query_bank, pin_bank), 1),
         )
 
     own, terms_f, terms_b, moving, fresh, sends = lax.cond(
         active, gather_and_multiply, gather_only
     )
 
-    sends, targets = sends
     pairs = sends.shape[1]
-    fresh = jnp.stack([fresh[place[replica]] for replica in range(replicas)])
     fresh = jnp.where(section == last, fresh, jnp.zeros_like(fresh))
     fresh = fresh.reshape(replicas * sections, col_width)
-    units = sends.reshape(2 * pairs, col_width)
-
-    def section_swap(units, fresh, reach):
-        message = jnp.concatenate([units, fresh])
+    known = [jnp.concatenate([sends.reshape(2 * pairs, col_width), fresh])]
+    offsets = [0]
+
+    def section_swap(reach):
+        offsets.extend([offset ^ reach for offset in offsets])
+        message = known[0] if len(known) == 1 else jnp.concatenate(known)
         other = lax.ppermute(message, "section", [(s, s ^ reach) for s in range(sections)])
-        return other
-
-    offsets = [0, sections // 2]
-    other = section_swap(units, fresh, sections // 2)
+        known.append(other)
+
+    section_swap(sections // 2)
 
     def reduce_middle(moving):
         f_top, f_low, b_top, b_low = moving
-        for distance in range(half - 1, 1, -1):
+        for distance in range(half - 2, 1, -1):
             to_f, to_b = terms_b[distance - 1], terms_f[distance - 1]
-            if distance < half - 1:
-                f_low, b_top = two_sums((to_f[1], f_low), (to_b[0], b_top))
-                f_low, b_top = forward(f_low), backward(b_top)
+            f_low, b_top = two_sums((to_f[1], f_low), (to_b[0], b_top))
+            f_low, b_top = forward(f_low), backward(b_top)
             f_top, b_low = two_sums((to_f[0], f_top), (to_b[1], b_low))
             f_top, b_low = forward(f_top), backward(b_low)
         return f_top, f_low, b_top, b_low
 
     moving = lax.cond(active, reduce_middle, lambda moving: moving, moving)
-    other, moving = lax.optimization_barrier((other, moving))
-    units = [units]
+    known[1], moving = lax.optimization_barrier((known[1], moving))
     reach = sections // 4
     while reach:
-        size = other.shape[0] - fresh.shape[0]
-        units, fresh = units + [other[:size]], fresh + other[size:]
-        other = section_swap(jnp.concatenate(units), fresh, reach)
-        offsets += [offset ^ reach for offset in offsets]
+        section_swap(reach)
         reach //= 2
     place_here = jnp.stack([me, section])
 
-    def loss(units, fresh, other):
+    def loss(known):
         grad = jax.ShapeDtypeStruct((pair_dev, col_width), jnp.float32)
         return pl.pallas_call(
             functools.partial(loss_kernel, offsets, replicas, pair_dev),
             out_shape=[grad, grad],
-            in_specs=[pl.BlockSpec(memory_space=pltpu.SMEM)] + [IN_VMEM] * (len(units) + 6),
+            in_specs=[pl.BlockSpec(memory_space=pltpu.SMEM)] + [IN_VMEM] * (len(known) + 2),
             out_specs=[IN_VMEM] * 2,
             compiler_params=pltpu.CompilerParams(vmem_limit_bytes=32 << 20),
-        )(place_here, *units, other, fresh, other, targets, query_bank, pin_bank)
-
-    def reduce_last(moving, units, fresh, other):
+        )(place_here, *known, query_bank, pin_bank)
+
+    def reduce_last(moving, known):
         f_top, f_low, b_top, b_low = moving
         to_f, to_b = terms_b[0], terms_f[0]
         f_low, b_top = two_sums((to_f[1], f_low), (to_b[0], b_top))
         f_low, b_top = forward(f_low), backward(b_top)
         f_top, b_low = two_sums((to_f[0], f_top), (to_b[1], b_low))
         f_top, b_low = forward(f_top), backward(b_low)
-        grads = loss(units, fresh, other)
+        grads = loss(known)
         plan = (
             (((0, 0), (1, 0), (3, 0), (5, 0)), 0, 0),
             (((0, cut), (2, 0), (4, 0), (6, 0)), 0, cut),
         )
         sources = [stream, *own, f_top, f_low, b_top, b_low]
-        return *sums(plan, sources, cut, [stream.shape]), *grads
-
-    def keep_stream(moving, units, fresh, other):
-        return stream + jnp.concatenate(own), *loss(units, fresh, other)
-
-    stream_out, grad_query, grad_pin = lax.cond(active, reduce_last, keep_stream, moving, units, fresh, other)
+        return *sums(plan, sources, cut, [stream.shape], pltpu.HBM), *grads
+
+    def keep_stream(moving, known):
+        return stream + jnp.concatenate(own), *loss(known)
+
+    stream_out, grad_query, grad_pin = lax.cond(active, reduce_last, keep_stream, moving, known)
     return (stream_out[None], grad_query, grad_pin)
 
 

time: 211 us -> 136 us (0.64)
  the two profiles are of different devices: /device:TPU:0 before, /device:TPU:11 now
where the time goes in v1:
time: 136 us; the launch traced here: 135 us
  Pallas kernels  49.5 us (36%)
  waiting for transfers between devices  43 us (32%)
  starting transfers between devices  33.9 us (25%)
  other arithmetic  4.12 us (3%)
  local copies, waits for them, and re-layouts  2.52 us (2%)
  between operations  1.59 us (1%)
    pallas_call x7, Pallas kernels, multiply(): pl.pallas_call(functools.partial(next_kernel, count), out_shape=out_shape...  23.9 us
    ppermute x14, starting transfers between devices, forward(): return lax.ppermute(values, 'dp', ring)  19.9 us
    ppermute x14, waiting for transfers between devices, forward(): return lax.ppermute(values, 'dp', ring)  18.6 us
    ppermute x3, waiting for transfers between devices, added_up(): values = values + lax.ppermute(values, BOTH, pairs)  10.9 us
    pallas_call x6, Pallas kernels, sums(): pl.pallas_call(functools.partial(sum_kernel, plan, len(sources)), out_sha...  9.85 us
    ppermute x14, waiting for transfers between devices, backward(): return lax.ppermute(values, 'dp', ring_back)  8.64 us
    pallas_call x1, Pallas kernels, multiply(): pl.pallas_call(functools.partial(first_kernel, count), out_shape=out_shap...  8.6 us
    ppermute x3, starting transfers between devices, added_up(): values = values + lax.ppermute(values, BOTH, pairs)  7.4 us
  transfers between devices with their start and end apart: 36, of which 19 were waited for; matrix products, arithmetic and copies ran while one was open for 2% of the time, Pallas kernels for 32%

profile of v1, /device:TPU:11, one launch (start us, length us, event | category | flops | bytes accessed | tf_op | source)
XLA Modules:
  0.0 135.4 jit_solution(882635539782342589)
XLA Ops:
  1.3 92.3 %conditional.8 = (bf16[64,4096]{1,0:T(8,128)(2,1)}, bf16[64,4096]{1,0:T(8,128)(2,1)}, bf16[64,4096]{1,0:T(8,128)(2,1)}, bf16[64,4096]{1,0:T(8,128)(2,1)}, bf16[6...) conditional(s32[]{:T(128)} %bitcast.12, ...), branch_computations={%region_0.3_spmd, %region_3.6_spmd} | conditional | flops 19330187264 | bytes 80091280
  1.3 2.5 %branch_1_fun.17 = (bf16[64,4096]{1,0:T(8,128)(2,1)S(1)}, bf16[64,4096]{1,0:T(8,128)(2,1)S(1)}) custom-call(bf16[128,4096]{1,0:T(8,128)(2,1)} %get-tuple-element.151.stream, bf16[1,4096]{1,0:T(2,128)(2,1)} %bitcast.29), custom_call_target="tpu_custom_call" | custom-call | tf_op jit(solution)/shard_map/cond/branch_1_fun/pallas_call | solution.py:172
  7.5 8.6 %branch_1_fun.18 = (bf16[64,4096]{1,0:T(8,128)(2,1)}, bf16[64,4096]{1,0:T(8,128)(2,1)}, f32[8,4096]{1,0:T(8,128)S(1)}, bf16[4096,768]{1,0:T(8,128)(2,1)S(1)}, bf...) custom-call(bf16[64,4096]{1,0:T(8,128)(2,1)S(1)} %get-tuple-element.153.refs_0_, ...), custom_call_target="tpu_custom_call" | custom-call | flops 2415919104 | bytes 2097152 | tf_op jit(solution)/shard_map/cond/branch_1_fun/pallas_call | solution.py:120
  17.5 2.7 %collective-permute-start.18 = (bf16[64,4096]{1,0:T(8,128)(2,1)S(1)}, bf16[64,4096]{1,0:T(8,128)(2,1)S(1)}, u32[]{:S(2)}, u32[]{:S(2)}) collective-permute-start(bf16[64,4096]{1,0:T(8,128)(2,1)S(1)} %collective-permute-done.14.refs_0_), channel_id=1, source_target_pairs={{0,8},{8,16},{16,24},{24,28},{28,20},{20,12},{12,4},{4,0},{1,9},{9... | collective-permute-start | bytes 1572872 | tf_op jit(solution)/shard_map/cond/branch_1_fun/ppermute | solution.py:381
  20.3 3.8 %branch_1_fun.19 = (bf16[64,4096]{1,0:T(8,128)(2,1)}, bf16[64,4096]{1,0:T(8,128)(2,1)}, f32[8,4096]{1,0:T(8,128)S(1)}) custom-call(bf16[64,4096]{1,0:T(8,128)(2,1)S(1)} %collective-permute-done.14.refs_0_, bf16[64,4096]{1,0:T(8,128)(2,1)S(1)} %collective-permute-done.15.refs_1_, bf16[4096,768]{1,0:T(8,128)(2,1)S(1)} %get-tuple-element.160.refs_2_, ...), custom_call_target="tpu_custom_call" | custom-call | flops 2415919104 | bytes 2097152 | tf_op jit(solution)/shard_map/cond/branch_1_fun/pallas_call | solution.py:131
  26.2 3.8 %branch_1_fun.20 = (bf16[64,4096]{1,0:T(8,128)(2,1)}, bf16[64,4096]{1,0:T(8,128)(2,1)}, f32[8,4096]{1,0:T(8,128)S(1)}) custom-call(bf16[64,4096]{1,0:T(8,128)(2,1)S(1)} %collective-permute-done.16.refs_0_, bf16[64,4096]{1,0:T(8,128)(2,1)S(1)} %collective-permute-done.17.refs_1_, bf16[4096,768]{1,0:T(8,128)(2,1)S(1)} %get-tuple-element.160.refs_2_, ...), custom_call_target="tpu_custom_call" | custom-call | flops 2415919104 | bytes 2097152 | tf_op jit(solution)/shard_map/cond/branch_1_fun/pallas_call | solution.py:131
  35.0 2.4 %collective-permute-done.20.refs_0_ = bf16[64,4096]{1,0:T(8,128)(2,1)S(1)} collective-permute-done((bf16[64,4096]{1,0:T(8,128)(2,1)S(1)}, bf16[64,4096]{1,0:T(8,128)(2,1)S(1)}, u32[]{:S(2)}, u32[]{:S(2)}) %collective-permute-start.20) | collective-permute-done | bytes 524320 | tf_op jit(solution)/shard_map/cond/branch_1_fun/ppermute | solution.py:381
  37.4 3.8 %branch_1_fun.22 = (bf16[64,4096]{1,0:T(8,128)(2,1)}, bf16[64,4096]{1,0:T(8,128)(2,1)}, f32[8,4096]{1,0:T(8,128)S(1)}) custom-call(bf16[64,4096]{1,0:T(8,128)(2,1)S(1)} %collective-permute-done.20.refs_0_, bf16[64,4096]{1,0:T(8,128)(2,1)S(1)} %collective-permute-done.21.refs_1_, bf16[4096,768]{1,0:T(8,128)(2,1)S(1)} %get-tuple-element.160.refs_2_, ...), custom_call_target="tpu_custom_call" | custom-call | flops 2415919104 | bytes 2097152 | tf_op jit(solution)/shard_map/cond/branch_1_fun/pallas_call | solution.py:131
  45.0 3.8 %branch_1_fun.21 = (bf16[64,4096]{1,0:T(8,128)(2,1)}, bf16[64,4096]{1,0:T(8,128)(2,1)}, f32[8,4096]{1,0:T(8,128)S(1)}) custom-call(bf16[64,4096]{1,0:T(8,128)(2,1)S(1)} %collective-permute-done.18.refs_0_, bf16[64,4096]{1,0:T(8,128)(2,1)S(1)} %collective-permute-done.19.refs_1_, bf16[4096,768]{1,0:T(8,128)(2,1)S(1)} %get-tuple-element.160.refs_2_, ...), custom_call_target="tpu_custom_call" | custom-call | flops 2415919104 | bytes 2097152 | tf_op jit(solution)/shard_map/cond/branch_1_fun/pallas_call | solution.py:131
  54.1 2.9 %branch_1_fun.24 = (bf16[64,4096]{1,0:T(8,128)(2,1)S(1)}, bf16[64,4096]{1,0:T(8,128)(2,1)S(1)}, f32[8,4096]{1,0:T(8,128)S(1)}) custom-call(bf16[64,4096]{1,0:T(8,128)(2,1)S(1)} %collective-permute-done.27.refs_0_, bf16[64,4096]{1,0:T(8,128)(2,1)S(1)} %collective-permute-done.28.refs_1_, bf16[4096,768]{1,0:T(8,128)(2,1)S(1)} %get-tuple-element.160.refs_2_, ...), custom_call_target="tpu_custom_call" | custom-call | flops 2415919104 | bytes 2097152 | tf_op jit(solution)/shard_map/cond/branch_1_fun/pallas_call | solution.py:131
  59.2 2.9 %branch_1_fun.26 = (bf16[64,4096]{1,0:T(8,128)(2,1)S(1)}, bf16[64,4096]{1,0:T(8,128)(2,1)S(1)}, f32[8,4096]{1,0:T(8,128)S(1)}) custom-call(bf16[64,4096]{1,0:T(8,128)(2,1)S(1)} %collective-permute-done.25.refs_0_, bf16[64,4096]{1,0:T(8,128)(2,1)S(1)} %collective-permute-done.26.refs_1_, bf16[4096,768]{1,0:T(8,128)(2,1)S(1)} %get-tuple-element.160.refs_2_, ...), custom_call_target="tpu_custom_call" | custom-call | flops 2415919104 | bytes 2097152 | tf_op jit(solution)/shard_map/cond/branch_1_fun/pallas_call | solution.py:131
  63.9 2.9 %branch_1_fun.23 = (bf16[64,4096]{1,0:T(8,128)(2,1)S(1)}, bf16[64,4096]{1,0:T(8,128)(2,1)S(1)}, f32[8,4096]{1,0:T(8,128)S(1)}) custom-call(bf16[64,4096]{1,0:T(8,128)(2,1)S(1)} %collective-permute-done.23.refs_0_, bf16[64,4096]{1,0:T(8,128)(2,1)S(1)} %collective-permute-done.24.refs_1_, bf16[4096,768]{1,0:T(8,128)(2,1)S(1)} %get-tuple-element.160.refs_2_, ...), custom_call_target="tpu_custom_call" | custom-call | flops 2415919104 | bytes 2097152 | tf_op jit(solution)/shard_map/cond/branch_1_fun/pallas_call | solution.py:131
  76.1 3.8 %collective-permute-done.37 = f32[8,4096]{1,0:T(8,128)S(1)} collective-permute-done((f32[8,4096]{1,0:T(8,128)}, f32[8,4096]{1,0:T(8,128)S(1)}, u32[]{:S(2)}, u32[]{:S(2)}) %collective-permute-start.37) | collective-permute-done | bytes 131104 | tf_op jit(solution)/shard_map/cond/branch_1_fun/ppermute | solution.py:406
  82.7 3.8 %collective-permute-done.38 = f32[8,4096]{1,0:T(8,128)S(1)} collective-permute-done((f32[8,4096]{1,0:T(8,128)S(1)}, f32[8,4096]{1,0:T(8,128)S(1)}, u32[]{:S(2)}, u32[]{:S(2)}) %collective-permute-start.38) | collective-permute-done | bytes 131104 | tf_op jit(solution)/shard_map/cond/branch_1_fun/ppermute | solution.py:406
  86.6 3.4 %collective-permute-start.39 = (f32[8,4096]{1,0:T(8,128)S(1)}, f32[8,4096]{1,0:T(8,128)S(1)}, u32[]{:S(2)}, u32[]{:S(2)}) collective-permute-start(f32[8,4096]{1,0:T(8,128)S(1)} %add.61), channel_id=1, source_target_pairs={{3,19},{7,23},{11,27},{15,31},{19,3},{23,7},{27,11},{31,15}} | collective-permute-start | bytes 393224 | tf_op jit(solution)/shard_map/cond/branch_1_fun/ppermute | solution.py:406
  90.0 3.3 %collective-permute-done.39 = f32[8,4096]{1,0:T(8,128)S(1)} collective-permute-done((f32[8,4096]{1,0:T(8,128)S(1)}, f32[8,4096]{1,0:T(8,128)S(1)}, u32[]{:S(2)}, u32[]{:S(2)}) %collective-permute-start.39) | collective-permute-done | bytes 131104 | tf_op jit(solution)/shard_map/cond/branch_1_fun/ppermute | solution.py:406
  94.9 17.0 %conditional.6 = ((bf16[64,4096]{1,0:T(8,128)(2,1)}, bf16[64,4096]{1,0:T(8,128)(2,1)}, bf16[64,4096]{1,0:T(8,128)(2,1)}, bf16[64,4096]{1,0:T(8,128)(2,1)})) conditional(s32[]{:T(128)} %bitcast.12, (bf16[64,4096]{1,0:T(8,128)(2,1)}, bf16[64,4096]{1,0:T(8,128)(2,1)}, bf16[64,4096]{1,0:T(8,128)(2,1)}, bf16[64,4096]{1,0:T(8,128)(2,1)}) %tuple.61, ...), branch_computations={%region_6.7_spmd, %region_7.8_spmd} | conditional | flops 2097152 | bytes 16777416 | solution.py:513
  101.4 3.5 %collective-permute-done = bf16[64,4096]{1,0:T(8,128)(2,1)} collective-permute-done((bf16[64,4096]{1,0:T(8,128)(2,1)S(1)}, bf16[64,4096]{1,0:T(8,128)(2,1)}, u32[]{:S(2)}, u32[]{:S(2)}) %collective-permute-start) | collective-permute-done | bytes 524320 | tf_op jit(solution)/shard_map/cond/branch_1_fun/ppermute | solution.py:381
  106.2 4.3 %collective-permute-done.1 = bf16[64,4096]{1,0:T(8,128)(2,1)} collective-permute-done((bf16[64,4096]{1,0:T(8,128)(2,1)S(1)}, bf16[64,4096]{1,0:T(8,128)(2,1)}, u32[]{:S(2)}, u32[]{:S(2)}) %collective-permute-start.1) | collective-permute-done | bytes 524320 | tf_op jit(solution)/shard_map/cond/branch_1_fun/ppermute | solution.py:381
  113.1 2.8 %collective-permute-done.41 = bf16[576,1024]{1,0:T(8,128)(2,1)S(1)} collective-permute-done((bf16[576,1024]{1,0:T(8,128)(2,1)S(1)}, bf16[576,1024]{1,0:T(8,128)(2,1)S(1)}, u32[]{:S(2)}, u32[]{:S(2)}) %collective-permute-start.41) | collective-permute-done | bytes 1179680 | tf_op jit(solution)/shard_map/ppermute | solution.py:498
  115.9 19.3 %conditional.7 = (f32[16,1024]{1,0:T(8,128)}, f32[16,1024]{1,0:T(8,128)}, bf16[1,128,4096]{2,1,0:T(8,128)(2,1)}) conditional(s32[]{:T(128)} %bitcast.12, (s32[2]{0:T(128)S(1)}, bf16[288,1024]{1,0:T(8,128)(2,1)S(1)}, bf16[288,1024]{1,0:T(8,128)(2,1)S(1)}, bf16[576,1024]{1,0:T(8,128)(2,1)S(1)}, bf16[16,4096]{1,0:T(8,128)(2,1)S(1)}, ...), branch_computations={%region_8.9_spmd, %region_9.10_spmd} | conditional | flops 4194304 | bytes 25166008 | solution.py:549
  122.4 2.7 %branch_1_fun.30 = (f32[16,1024]{1,0:T(8,128)}, f32[16,1024]{1,0:T(8,128)}) custom-call(s32[2]{0:T(128)S(1)} %get-tuple-element.243.where_ref, bf16[288,1024]{1,0:T(8,128)(2,1)S(1)} %get-tuple-element.244.refs_0_, bf16[288,1024]{1,0:T(8,128)(2,1)S(1)} %get-tuple-element.245.refs_1_, bf16[576,1024]{1,0:T(8,128)(2,1)S(1)} %get-tuple-element.246.refs_2_, ...), custom_call_target="tpu_custom_call" | custom-call | tf_op jit(solution)/shard_map/cond/branch_1_fun/pallas_call | solution.py:523
  127.2 4.2 %collective-permute-done.5.refs_4_ = bf16[64,4096]{1,0:T(8,128)(2,1)S(1)} collective-permute-done((bf16[64,4096]{1,0:T(8,128)(2,1)S(1)}, bf16[64,4096]{1,0:T(8,128)(2,1)S(1)}, u32[]{:S(2)}, u32[]{:S(2)}) %collective-permute-start.5) | collective-permute-done | bytes 524320 | tf_op jit(solution)/shard_map/cond/branch_1_fun/ppermute | solution.py:381
  132.8 2.4 %branch_1_fun.33 = bf16[128,4096]{1,0:T(8,128)(2,1)} custom-call(bf16[128,4096]{1,0:T(8,128)(2,1)S(1)} %get-tuple-element.251.refs_0_, bf16[64,4096]{1,0:T(8,128)(2,1)} %get-tuple-element.252.refs_1_, bf16[64,4096]{1,0:T(8,128)(2,1)} %get-tuple-element.253.refs_2_, bf16[64,4096]{1,0:T(8,128)(2,1)S(1)} %collective-permute-done.4.refs_3_, ...), custom_call_target="tpu_custom_call" | custom-call | flops 2097152 | bytes 8388608 | tf_op jit(solution)/shard_map/cond/branch_1_fun/pallas_call | solution.py:231
  (121 shorter events, 58.9 us)
Async XLA Ops:
  3.8 20.9 %collective-permute-start.17 = (bf16[64,4096]{1,0:T(8,128)(2,1)S(1)}, bf16[64,4096]{1,0:T(8,128)(2,1)S(1)}, u32[]{:S(2)}, u32[]{:S(2)}) collective-permute-start(bf16[64,4096]{1,0:T(8,128)(2,1)S(1)} %get-tuple-element.153.refs_0_), channel_id=1, source_target_pairs={{8,0},{16,8},{24,16},{28,24},{20,28},{12,20},{4,12},{0,4},{9,1},{1... | collective-permute-start | bytes 1572872 | tf_op jit(solution)/shard_map/cond/branch_1_fun/ppermute | solution.py:384
  4.1 12.4 %collective-permute-start.14 = (bf16[64,4096]{1,0:T(8,128)(2,1)S(1)}, bf16[64,4096]{1,0:T(8,128)(2,1)S(1)}, u32[]{:S(2)}, u32[]{:S(2)}) collective-permute-start(bf16[64,4096]{1,0:T(8,128)(2,1)S(1)} %get-tuple-element.153.refs_0_), channel_id=1, source_target_pairs={{0,8},{8,16},{16,24},{24,28},{28,20},{20,12},{12,4},{4,0},{1,9},{9... | collective-permute-start | bytes 1572872 | tf_op jit(solution)/shard_map/cond/branch_1_fun/ppermute | solution.py:381
  5.4 19.4 %collective-permute-start.16 = (bf16[64,4096]{1,0:T(8,128)(2,1)S(1)}, bf16[64,4096]{1,0:T(8,128)(2,1)S(1)}, u32[]{:S(2)}, u32[]{:S(2)}) collective-permute-start(bf16[64,4096]{1,0:T(8,128)(2,1)S(1)} %get-tuple-element.154.refs_1_), channel_id=1, source_target_pairs={{0,8},{8,16},{16,24},{24,28},{28,20},{20,12},{12,4},{4,0},{1,9},{9... | collective-permute-start | bytes 1572872 | tf_op jit(solution)/shard_map/cond/branch_1_fun/ppermute | solution.py:381
  6.6 10.9 %collective-permute-start.15 = (bf16[64,4096]{1,0:T(8,128)(2,1)S(1)}, bf16[64,4096]{1,0:T(8,128)(2,1)S(1)}, u32[]{:S(2)}, u32[]{:S(2)}) collective-permute-start(bf16[64,4096]{1,0:T(8,128)(2,1)S(1)} %get-tuple-element.154.refs_1_), channel_id=1, source_target_pairs={{8,0},{16,8},{24,16},{28,24},{20,28},{12,20},{4,12},{0,4},{9,1},{1... | collective-permute-start | bytes 1572872 | tf_op jit(solution)/shard_map/cond/branch_1_fun/ppermute | solution.py:384
  17.5 14.2 %collective-permute-start.18 = (bf16[64,4096]{1,0:T(8,128)(2,1)S(1)}, bf16[64,4096]{1,0:T(8,128)(2,1)S(1)}, u32[]{:S(2)}, u32[]{:S(2)}) collective-permute-start(bf16[64,4096]{1,0:T(8,128)(2,1)S(1)} %collective-permute-done.14.refs_0_), channel_id=1, source_target_pairs={{0,8},{8,16},{16,24},{24,28},{28,20},{20,12},{12,4},{4,0},{1,9},{9... | collective-permute-start | bytes 1572872 | tf_op jit(solution)/shard_map/cond/branch_1_fun/ppermute | solution.py:381
  20.2 11.5 %collective-permute-start.19 = (bf16[64,4096]{1,0:T(8,128)(2,1)S(1)}, bf16[64,4096]{1,0:T(8,128)(2,1)S(1)}, u32[]{:S(2)}, u32[]{:S(2)}) collective-permute-start(bf16[64,4096]{1,0:T(8,128)(2,1)S(1)} %collective-permute-done.15.refs_1_), channel_id=1, source_target_pairs={{8,0},{16,8},{24,16},{28,24},{20,28},{12,20},{4,12},{0,4},{9,1},{1... | collective-permute-start | bytes 1572872 | tf_op jit(solution)/shard_map/cond/branch_1_fun/ppermute | solution.py:384
  24.8 12.6 %collective-permute-start.20 = (bf16[64,4096]{1,0:T(8,128)(2,1)S(1)}, bf16[64,4096]{1,0:T(8,128)(2,1)S(1)}, u32[]{:S(2)}, u32[]{:S(2)}) collective-permute-start(bf16[64,4096]{1,0:T(8,128)(2,1)S(1)} %collective-permute-done.16.refs_0_), channel_id=1, source_target_pairs={{0,8},{8,16},{16,24},{24,28},{28,20},{20,12},{12,4},{4,0},{1,9},{9... | collective-permute-start | bytes 1572872 | tf_op jit(solution)/shard_map/cond/branch_1_fun/ppermute | solution.py:381
  26.2 11.1 %collective-permute-start.21 = (bf16[64,4096]{1,0:T(8,128)(2,1)S(1)}, bf16[64,4096]{1,0:T(8,128)(2,1)S(1)}, u32[]{:S(2)}, u32[]{:S(2)}) collective-permute-start(bf16[64,4096]{1,0:T(8,128)(2,1)S(1)} %collective-permute-done.17.refs_1_), channel_id=1, source_target_pairs={{8,0},{16,8},{24,16},{28,24},{20,28},{12,20},{4,12},{0,4},{9,1},{1... | collective-permute-start | bytes 1572872 | tf_op jit(solution)/shard_map/cond/branch_1_fun/ppermute | solution.py:384
  31.8 11.2 %collective-permute-start.25 = (bf16[64,4096]{1,0:T(8,128)(2,1)S(1)}, bf16[64,4096]{1,0:T(8,128)(2,1)S(1)}, u32[]{:S(2)}, u32[]{:S(2)}) collective-permute-start(bf16[64,4096]{1,0:T(8,128)(2,1)S(1)} %collective-permute-done.18.refs_0_), channel_id=1, source_target_pairs={{0,8},{8,16},{16,24},{24,28},{28,20},{20,12},{12,4},{4,0},{1,9},{9... | collective-permute-start | bytes 1572872 | tf_op jit(solution)/shard_map/cond/branch_1_fun/ppermute | solution.py:381
  33.8 11.1 %collective-permute-start.22 = (bf16[2,16,1024]{2,1,0:T(8,128)(2,1)S(1)}, bf16[2,16,1024]{2,1,0:T(8,128)(2,1)S(1)}, u32[]{:S(2)}, u32[]{:S(2)}) collective-permute-start(bf16[2,16,1024]{2,1,0:T(8,128)(2,1)S(1)} %pad_maximum_fusion.5), channel_id=1, source_target_pairs={{0,4},{4,0},{8,12},{12,8},{16,20},{20,16},{24,28},{28,24},{1,5},{5... | collective-permute-start | bytes 196616 | tf_op jit(solution)/shard_map/cond/branch_1_fun/ppermute | solution.py:393
  43.0 11.1 %collective-permute-start.27 = (bf16[64,4096]{1,0:T(8,128)(2,1)S(1)}, bf16[64,4096]{1,0:T(8,128)(2,1)S(1)}, u32[]{:S(2)}, u32[]{:S(2)}) collective-permute-start(bf16[64,4096]{1,0:T(8,128)(2,1)S(1)} %collective-permute-done.25.refs_0_), channel_id=1, source_target_pairs={{0,8},{8,16},{16,24},{24,28},{28,20},{20,12},{12,4},{4,0},{1,9},{9... | collective-permute-start | bytes 1572872 | tf_op jit(solution)/shard_map/cond/branch_1_fun/ppermute | solution.py:381
  48.8 13.3 %collective-permute-start.23 = (bf16[64,4096]{1,0:T(8,128)(2,1)S(1)}, bf16[64,4096]{1,0:T(8,128)(2,1)S(1)}, u32[]{:S(2)}, u32[]{:S(2)}) collective-permute-start(bf16[64,4096]{1,0:T(8,128)(2,1)S(1)} %collective-permute-done.20.refs_0_), channel_id=1, source_target_pairs={{0,8},{8,16},{16,24},{24,28},{28,20},{20,12},{12,4},{4,0},{1,9},{9... | collective-permute-start | bytes 1572872 | tf_op jit(solution)/shard_map/cond/branch_1_fun/ppermute | solution.py:381
  50.3 13.3 %collective-permute-start.24 = (bf16[64,4096]{1,0:T(8,128)(2,1)S(1)}, bf16[64,4096]{1,0:T(8,128)(2,1)S(1)}, u32[]{:S(2)}, u32[]{:S(2)}) collective-permute-start(bf16[64,4096]{1,0:T(8,128)(2,1)S(1)} %collective-permute-done.21.refs_1_), channel_id=1, source_target_pairs={{8,0},{16,8},{24,16},{28,24},{20,28},{12,20},{4,12},{0,4},{9,1},{1... | collective-permute-start | bytes 1572872 | tf_op jit(solution)/shard_map/cond/branch_1_fun/ppermute | solution.py:384
  52.5 14.4 %collective-permute-start.32 = (bf16[2,64,1024]{2,1,0:T(8,128)(2,1)S(1)}, bf16[2,64,1024]{2,1,0:T(8,128)(2,1)S(1)}, u32[]{:S(2)}, u32[]{:S(2)}) collective-permute-start(bf16[2,64,1024]{2,1,0:T(8,128)(2,1)S(1)} %constant_dynamic-update-slice_fusion.2), channel_id=1, source_target_pairs={{0,16},{4,20},{8,24},{12,28},{16,0},{20,4},{24,8},{28,12},{1,17},{... | collective-permute-start | bytes 786440 | tf_op jit(solution)/shard_map/cond/branch_1_fun/ppermute | solution.py:393
  59.2 10.7 %collective-permute-start.30 = (bf16[64,4096]{1,0:T(8,128)(2,1)S(1)}, bf16[64,4096]{1,0:T(8,128)(2,1)S(1)}, u32[]{:S(2)}, u32[]{:S(2)}) collective-permute-start(bf16[64,4096]{1,0:T(8,128)(2,1)S(1)} %get-tuple-element.190), channel_id=1, source_target_pairs={{8,0},{16,8},{24,16},{28,24},{20,28},{12,20},{4,12},{0,4},{9,1},{1... | collective-permute-start | bytes 1572872 | tf_op jit(solution)/shard_map/cond/branch_1_fun/ppermute | solution.py:384
  62.1 31.2 %collective-permute-start.34 = (bf16[64,4096]{1,0:T(8,128)(2,1)S(1)}, bf16[64,4096]{1,0:T(8,128)(2,1)}, u32[]{:S(2)}, u32[]{:S(2)}) collective-permute-start(bf16[64,4096]{1,0:T(8,128)(2,1)S(1)} %get-tuple-element.199), channel_id=1, source_target_pairs={{0,8},{8,16},{16,24},{24,28},{28,20},{20,12},{12,4},{4,0},{1,9},{9... | collective-permute-start | bytes 1572872 | tf_op jit(solution)/shard_map/cond/branch_1_fun/ppermute | solution.py:381
  63.6 29.7 %collective-permute-start.35 = (bf16[64,4096]{1,0:T(8,128)(2,1)S(1)}, bf16[64,4096]{1,0:T(8,128)(2,1)}, u32[]{:S(2)}, u32[]{:S(2)}) collective-permute-start(bf16[64,4096]{1,0:T(8,128)(2,1)S(1)} %get-tuple-element.200), channel_id=1, source_target_pairs={{8,0},{16,8},{24,16},{28,24},{20,28},{12,20},{4,12},{0,4},{9,1},{1... | collective-permute-start | bytes 1572872 | tf_op jit(solution)/shard_map/cond/branch_1_fun/ppermute | solution.py:384
  70.5 22.8 %collective-permute-start.33 = (bf16[64,4096]{1,0:T(8,128)(2,1)S(1)}, bf16[64,4096]{1,0:T(8,128)(2,1)}, u32[]{:S(2)}, u32[]{:S(2)}) collective-permute-start(bf16[64,4096]{1,0:T(8,128)(2,1)S(1)} %get-tuple-element.196), channel_id=1, source_target_pairs={{0,8},{8,16},{16,24},{24,28},{28,20},{20,12},{12,4},{4,0},{1,9},{9... | collective-permute-start | bytes 1572872 | tf_op jit(solution)/shard_map/cond/branch_1_fun/ppermute | solution.py:381
  70.6 22.8 %collective-permute-start.36 = (bf16[64,4096]{1,0:T(8,128)(2,1)S(1)}, bf16[64,4096]{1,0:T(8,128)(2,1)}, u32[]{:S(2)}, u32[]{:S(2)}) collective-permute-start(bf16[64,4096]{1,0:T(8,128)(2,1)S(1)} %get-tuple-element.201), channel_id=1, source_target_pairs={{8,0},{16,8},{24,16},{28,24},{20,28},{12,20},{4,12},{0,4},{9,1},{1... | collective-permute-start | bytes 1572872 | tf_op jit(solution)/shard_map/cond/branch_1_fun/ppermute | solution.py:384
  94.8 17.1 %collective-permute-start.40 = (bf16[288,1024]{1,0:T(8,128)(2,1)S(1)}, bf16[288,1024]{1,0:T(8,128)(2,1)S(1)}, u32[]{:S(2)}, u32[]{:S(2)}) collective-permute-start(bf16[288,1024]{1,0:T(8,128)(2,1)S(1)} %constant_dynamic-update-slice_fusion.4), channel_id=1, source_target_pairs={{0,2},{1,3},{2,0},{3,1},{4,6},{5,7},{6,4},{7,5},{8,10},{9,11},{10,... | collective-permute-start | bytes 1769480 | tf_op jit(solution)/shard_map/ppermute | solution.py:498
  99.9 10.6 %collective-permute-start.1 = (bf16[64,4096]{1,0:T(8,128)(2,1)S(1)}, bf16[64,4096]{1,0:T(8,128)(2,1)}, u32[]{:S(2)}, u32[]{:S(2)}) collective-permute-start(bf16[64,4096]{1,0:T(8,128)(2,1)S(1)} %get-tuple-element.229), channel_id=1, source_target_pairs={{0,8},{8,16},{16,24},{24,28},{28,20},{20,12},{12,4},{4,0},{1,9},{9... | collective-permute-start | bytes 1572872 | tf_op jit(solution)/shard_map/cond/branch_1_fun/ppermute | solution.py:381
  101.3 10.5 %collective-permute-start.2 = (bf16[64,4096]{1,0:T(8,128)(2,1)S(1)}, bf16[64,4096]{1,0:T(8,128)(2,1)}, u32[]{:S(2)}, u32[]{:S(2)}) collective-permute-start(bf16[64,4096]{1,0:T(8,128)(2,1)S(1)} %get-tuple-element.230), channel_id=1, source_target_pairs={{8,0},{16,8},{24,16},{28,24},{20,28},{12,20},{4,12},{0,4},{9,1},{1... | collective-permute-start | bytes 1572872 | tf_op jit(solution)/shard_map/cond/branch_1_fun/ppermute | solution.py:384
  120.8 10.5 %collective-permute-start.5 = (bf16[64,4096]{1,0:T(8,128)(2,1)S(1)}, bf16[64,4096]{1,0:T(8,128)(2,1)S(1)}, u32[]{:S(2)}, u32[]{:S(2)}) collective-permute-start(bf16[64,4096]{1,0:T(8,128)(2,1)S(1)} %get-tuple-element.263), channel_id=1, source_target_pairs={{0,8},{8,16},{16,24},{24,28},{28,20},{20,12},{12,4},{4,0},{1,9},{9... | collective-permute-start | bytes 1572872 | tf_op jit(solution)/shard_map/cond/branch_1_fun/ppermute | solution.py:381
  122.4 10.4 %collective-permute-start.6 = (bf16[64,4096]{1,0:T(8,128)(2,1)S(1)}, bf16[64,4096]{1,0:T(8,128)(2,1)S(1)}, u32[]{:S(2)}, u32[]{:S(2)}) collective-permute-start(bf16[64,4096]{1,0:T(8,128)(2,1)S(1)} %get-tuple-element.264), channel_id=1, source_target_pairs={{8,0},{16,8},{24,16},{28,24},{20,28},{12,20},{4,12},{0,4},{9,1},{1... | collective-permute-start | bytes 1572872 | tf_op jit(solution)/shard_map/cond/branch_1_fun/ppermute | solution.py:384
  (26 other events, 221.3 us)
